TPU v7x, 32 devices: a whole 2x2x4 slice. The times are simulated.
32 devices in a mesh: gx: 8 (over z, y), gz: 4 (over x, core).
Axes of the slice: x: 2, y: 2, z: 4, core: 2. Of those that a mesh axis runs over, the one named last changes fastest.
Arguments:
- populations: float32 [19, 32, 64, 128], P(None, 'gx', 'gz'), may hold values from 0.019 to 0.44, as said below
- fluid_mask: int32 [32, 64, 128], P('gx', 'gz'), may hold values 0 or 1
Outputs:
- spectrum: float32 [2, 128, 32, 64], P(None, 'gx', 'gz')
Inputs may be any that keep to these rules, and one draw needn't show every extreme that they name: `populations`: each entry lies between 0.7 and 1.3 times the weight of its velocity.
All inputs are finite; a program needn't handle non-finite values. No bound on the sum of `fluid_mask` on one device may be relied on, other than what follows from the above.
Results may differ from a plain program's by a relative error of at most 0.0003.
Values sent between devices are 32-bit elements; how exact they have to be, the bound alone decides.
A program may use at most 64 MiB of HBM per device.

v0:
```python
import math

import jax
import jax.numpy as jnp
from jax import lax
from jax.sharding import PartitionSpec as P

VELOCITIES = (
    (0, 0, 0),
    (1, 0, 0),
    (-1, 0, 0),
    (0, 1, 0),
    (0, -1, 0),
    (0, 0, 1),
    (0, 0, -1),
    (1, 1, 0),
    (-1, -1, 0),
    (1, -1, 0),
    (-1, 1, 0),
    (1, 0, 1),
    (-1, 0, -1),
    (1, 0, -1),
    (-1, 0, 1),
    (0, 1, 1),
    (0, -1, -1),
    (0, 1, -1),
    (0, -1, 1),
)
LATTICE_WEIGHTS = (1.0 / 3.0,) + (1.0 / 18.0,) * 6 + (1.0 / 36.0,) * 12
OPPOSITES = (0, 2, 1, 4, 3, 6, 5, 8, 7, 10, 9, 12, 11, 14, 13, 16, 15, 18, 17)
RELAX_TIME = 0.6
BODY_FORCE = 0.0001
SPEED_UNIT = 0.05


def with_halo(cells, sides, width):
    for axis, dim in sides:
        count = lax.axis_size(axis)
        head = lax.slice_in_dim(cells, 0, width, axis=dim)
        tail = lax.slice_in_dim(cells, cells.shape[dim] - width, cells.shape[dim], axis=dim)
        cells = jnp.concatenate(
            [
                lax.ppermute(tail, axis, [(i, (i + 1) % count) for i in range(count)]),
                cells,
                lax.ppermute(head, axis, [((i + 1) % count, i) for i in range(count)]),
            ],
            axis=dim,
        )
    return cells


def component(which, float_type):
    return jnp.asarray([velocity[which] for velocity in VELOCITIES], float_type).reshape(
        19, 1, 1, 1
    )


def collide(current, fluid_cells):
    float_type = current.dtype
    along_x = component(0, float_type)
    along_y = component(1, float_type)
    along_z = component(2, float_type)
    weights = jnp.asarray(LATTICE_WEIGHTS, float_type).reshape(19, 1, 1, 1)
    density = jnp.sum(current, axis=0)
    speed_x = jnp.sum(along_x * current, axis=0) / density
    speed_y = jnp.sum(along_y * current, axis=0) / density
    speed_z = jnp.sum(along_z * current, axis=0) / density
    project = along_x * speed_x + along_y * speed_y + along_z * speed_z
    square = speed_x * speed_x + speed_y * speed_y + speed_z * speed_z
    balance = weights * density * (1.0 + 3.0 * project + 4.5 * project * project - 1.5 * square)
    relaxed = (
        current - (current - balance) / RELAX_TIME + 3.0 * BODY_FORCE * weights * along_x * density
    )
    return jnp.where(fluid_cells > 0, relaxed, current)


def stream(padded):
    extent_x = padded.shape[1] - 2
    extent_z = padded.shape[2] - 2
    height = padded.shape[3]
    walled = jnp.pad(padded, ((0, 0), (0, 0), (0, 0), (1, 1)))
    fluid_self = padded[19, 1 : 1 + extent_x, 1 : 1 + extent_z, :]
    results = []
    for number in range(19):
        step_x, step_y, step_z = VELOCITIES[number]
        start_x = 1 - step_x
        start_z = 1 - step_z
        start_y = 1 - step_y
        source_value = walled[
            number,
            start_x : start_x + extent_x,
            start_z : start_z + extent_z,
            start_y : start_y + height,
        ]
        source_fluid = walled[
            19,
            start_x : start_x + extent_x,
            start_z : start_z + extent_z,
            start_y : start_y + height,
        ]
        bounce = padded[OPPOSITES[number], 1 : 1 + extent_x, 1 : 1 + extent_z, :]
        own_value = padded[number, 1 : 1 + extent_x, 1 : 1 + extent_z, :]
        arrived = jnp.where(source_fluid > 0, source_value, bounce)
        results.append(jnp.where(fluid_self > 0, arrived, own_value))
    return jnp.stack(results, axis=0)


def dft_tables(length, factor):
    index = jnp.arange(length, dtype=jnp.int32)
    products = index[:, None] * index[None, :] % length
    angles = products.astype(jnp.float32) * (2.0 * math.pi / length)
    return (jnp.cos(angles) * factor, jnp.sin(angles) * factor)


def shards(populations, fluid_mask):
    fluid_cells = fluid_mask.astype(jnp.float32)
    current = populations
    for repeat in range(2):
        relaxed = collide(current, fluid_cells)
        stacked = jnp.concatenate([relaxed, fluid_cells[None]], axis=0)
        padded = with_halo(stacked, (("gx", 1), ("gz", 2)), 1)
        current = stream(padded)
    along_x = component(0, jnp.float32)
    density = jnp.sum(current, axis=0)
    speed_x = fluid_cells * jnp.sum(along_x * current, axis=0) / density
    columns = jnp.transpose(speed_x, (2, 1, 0))
    full_x = speed_x.shape[0] * lax.axis_size("gx")
    full_z = speed_x.shape[1] * lax.axis_size("gz")
    norm_scale = 1.0 / (math.sqrt(full_x * full_z) * SPEED_UNIT)
    highest = lax.Precision.HIGHEST
    block = lax.all_to_all(columns, "gx", split_axis=0, concat_axis=2, tiled=True)
    cosine, sine = dft_tables(block.shape[2], norm_scale)
    real_part = jnp.einsum("yzx,xk->yzk", block, cosine, precision=highest)
    imag_part = -jnp.einsum("yzx,xk->yzk", block, sine, precision=highest)
    along_kx = jnp.stack([real_part, imag_part], axis=0)
    block = lax.all_to_all(along_kx, "gz", split_axis=3, concat_axis=2, tiled=True)
    cosine, sine = dft_tables(block.shape[2], 1.0)
    real_in = block[0]
    imag_in = block[1]
    real_part = jnp.einsum("ync,nk->yck", real_in, cosine, precision=highest) + jnp.einsum(
        "ync,nk->yck", imag_in, sine, precision=highest
    )
    imag_part = jnp.einsum("ync,nk->yck", imag_in, cosine, precision=highest) - jnp.einsum(
        "ync,nk->yck", real_in, sine, precision=highest
    )
    return jnp.stack([real_part, imag_part], axis=0)


def solution(mesh):
    placed = (P(None, "gx", "gz", None), P("gx", "gz", None))
    return jax.shard_map(
        shards, mesh=mesh, in_specs=placed, out_specs=P(None, "gx", "gz", None), check_vma=False
    )
```

profile of v0, /device:TPU:0, one launch (start us, length us, event | category | flops | bytes accessed | tf_op | source)
XLA Modules:
  0.0 65.3 jit_solution(15771137389065080716)
XLA Ops:
  0.0 0.8 %convert_compare_fusion = pred[4,16,128]{2,1,0:T(8,128)(4,1)S(1)} fusion(s32[4,16,128]{2,1,0:T(8,128)} %param.12), kind=kLoop, calls=%fused_computation.383 | loop fusion | flops 16384 | bytes 40960 | tf_op jit(solution)/shard_map/gt | solution.py:104
  0.8 0.8 %convert_bitcast_fusion = f32[1,4,16,128]{3,2,1,0:T(8,128)S(1)} fusion(s32[4,16,128]{2,1,0:T(8,128)} %param.12), kind=kLoop, calls=%fused_computation.382 | loop fusion | flops 8192 | bytes 65536 | tf_op jit(solution)/shard_map/broadcast_in_dim | solution.py:120
  1.6 1.3 %multiply_reduce_fusion.6 = (f32[4,16,128]{2,1,0:T(8,128)S(1)}, f32[4,16,128]{2,1,0:T(8,128)S(1)}, f32[4,16,128]{2,1,0:T(8,128)S(1)}, f32[4,16,128]{2,1,0:T(8,128)S(1)}) fusion(f32[19,4,16,128]{3,2,1,0:T(8,128)} %param.11, f32[19]{0:T(128)} %constant.62.clone, f32[19]{0:T(128)} %constant.63.clone, f32[19]{0:T(128)} %constant.64.clone), kind=kLoop, calls=%fused_computation.114 | loop fusion | flops 1056768 | bytes 753892 | tf_op jit(solution)/shard_map/reduce_sum | solution.py:65
  3.0 1.2 %fusion.38 = f32[19,4,16,128]{3,2,1,0:T(8,128)S(1)} fusion(f32[19,4,16,128]{3,2,1,0:T(8,128)S(1)} %copy-done.1, f32[19]{0:T(128)} %constant.73, f32[4,16,128]{2,1,0:T(8,128)S(1)} %get-tuple-element.46, f32[4,16,128]{2,1,0:T(8,128)S(1)} %get-tuple-element.49, f32[19]{0:T(128)} %constant.64.clone, f32[4,16,128]{2,1,0:T(8,128)S(1)} %get-tuple-element.48, ...), kind=kLoop, calls=%fused_computation.99 | loop fusion | flops 2957312 | bytes 1417596 | tf_op jit(solution)/shard_map/jit(_where)/select_n | solution.py:74
  4.2 6.1 %collective-permute-start.1 = (f32[20,1,16,128]{3,2,1,0:T(8,128)S(1)}, f32[20,1,16,128]{3,2,1,0:T(8,128)S(1)}, u32[]{:S(2)}, u32[]{:S(2)}) collective-permute-start(f32[20,1,16,128]{3,2,1,0:T(8,128)S(1)} %get-tuple-element.64), channel_id=1, source_target_pairs={{4,0},{8,4},{12,8},{16,12},{20,16},{24,20},{28,24},{0,28},{5,1},{9... | collective-permute-start | bytes 491528 | tf_op jit(solution)/shard_map/ppermute | solution.py:45
  10.3 3.5 %collective-permute-done.1 = f32[20,1,16,128]{3,2,1,0:T(8,128)S(1)} collective-permute-done((f32[20,1,16,128]{3,2,1,0:T(8,128)S(1)}, f32[20,1,16,128]{3,2,1,0:T(8,128)S(1)}, u32[]{:S(2)}, u32[]{:S(2)}) %collective-permute-start.1) | collective-permute-done | bytes 163872 | tf_op jit(solution)/shard_map/ppermute | solution.py:45
  13.7 4.9 %collective-permute-done = f32[20,1,16,128]{3,2,1,0:T(8,128)S(1)} collective-permute-done((f32[20,1,16,128]{3,2,1,0:T(8,128)S(1)}, f32[20,1,16,128]{3,2,1,0:T(8,128)S(1)}, u32[]{:S(2)}, u32[]{:S(2)}) %collective-permute-start) | collective-permute-done | bytes 163872 | tf_op jit(solution)/shard_map/ppermute | solution.py:43
  18.9 0.5 collective-permute-start.2
  19.5 1.2 %collective-permute-done.3 = f32[20,6,1,128]{3,2,1,0:T(1,128)S(1)} collective-permute-done((f32[20,6,1,128]{3,2,1,0:T(1,128)S(1)}, f32[20,6,1,128]{3,2,1,0:T(1,128)S(1)}, u32[]{:S(2)}, u32[]{:S(2)}) %collective-permute-start.3) | collective-permute-done | bytes 61472 | tf_op jit(solution)/shard_map/ppermute | solution.py:45
  20.7 2.5 %collective-permute-done.2 = f32[20,6,1,128]{3,2,1,0:T(1,128)S(1)} collective-permute-done((f32[20,6,1,128]{3,2,1,0:T(1,128)S(1)}, f32[20,6,1,128]{3,2,1,0:T(1,128)S(1)}, u32[]{:S(2)}, u32[]{:S(2)}) %collective-permute-start.2) | collective-permute-done | bytes 61472 | tf_op jit(solution)/shard_map/ppermute | solution.py:43
  24.8 0.4 copy-done.2
  25.9 0.5 fusion.46
  26.5 1.4 %collective-permute-start.5 = (f32[20,1,16,128]{3,2,1,0:T(8,128)S(1)}, f32[20,1,16,128]{3,2,1,0:T(8,128)S(1)}, u32[]{:S(2)}, u32[]{:S(2)}) collective-permute-start(f32[20,1,16,128]{3,2,1,0:T(8,128)S(1)} %get-tuple-element.60), channel_id=1, source_target_pairs={{4,0},{8,4},{12,8},{16,12},{20,16},{24,20},{28,24},{0,28},{5,1},{9... | collective-permute-start | bytes 491528 | tf_op jit(solution)/shard_map/ppermute | solution.py:45
  27.9 0.7 %collective-permute-start.4 = (f32[20,1,16,128]{3,2,1,0:T(8,128)S(1)}, f32[20,1,16,128]{3,2,1,0:T(8,128)S(1)}, u32[]{:S(2)}, u32[]{:S(2)}) collective-permute-start(f32[20,1,16,128]{3,2,1,0:T(8,128)S(1)} %get-tuple-element.61), channel_id=1, source_target_pairs={{0,4},{4,8},{8,12},{12,16},{16,20},{20,24},{24,28},{28,0},{1,5},{5... | collective-permute-start | bytes 491528 | tf_op jit(solution)/shard_map/ppermute | solution.py:43
  28.6 4.2 %collective-permute-done.5 = f32[20,1,16,128]{3,2,1,0:T(8,128)S(1)} collective-permute-done((f32[20,1,16,128]{3,2,1,0:T(8,128)S(1)}, f32[20,1,16,128]{3,2,1,0:T(8,128)S(1)}, u32[]{:S(2)}, u32[]{:S(2)}) %collective-permute-start.5) | collective-permute-done | bytes 163872 | tf_op jit(solution)/shard_map/ppermute | solution.py:45
  32.7 3.7 %collective-permute-done.4 = f32[20,1,16,128]{3,2,1,0:T(8,128)S(1)} collective-permute-done((f32[20,1,16,128]{3,2,1,0:T(8,128)S(1)}, f32[20,1,16,128]{3,2,1,0:T(8,128)S(1)}, u32[]{:S(2)}, u32[]{:S(2)}) %collective-permute-start.4) | collective-permute-done | bytes 163872 | tf_op jit(solution)/shard_map/ppermute | solution.py:43
  36.7 0.5 collective-permute-start.6
  37.4 1.7 %collective-permute-done.7 = f32[20,6,1,128]{3,2,1,0:T(1,128)S(1)} collective-permute-done((f32[20,6,1,128]{3,2,1,0:T(1,128)S(1)}, f32[20,6,1,128]{3,2,1,0:T(1,128)S(1)}, u32[]{:S(2)}, u32[]{:S(2)}) %collective-permute-start.7) | collective-permute-done | bytes 61472 | tf_op jit(solution)/shard_map/ppermute | solution.py:45
  39.1 1.3 %collective-permute-done.6 = f32[20,6,1,128]{3,2,1,0:T(1,128)S(1)} collective-permute-done((f32[20,6,1,128]{3,2,1,0:T(1,128)S(1)}, f32[20,6,1,128]{3,2,1,0:T(1,128)S(1)}, u32[]{:S(2)}, u32[]{:S(2)}) %collective-permute-start.6) | collective-permute-done | bytes 61472 | tf_op jit(solution)/shard_map/ppermute | solution.py:43
  42.7 9.1 %all_to_all.33 = f32[8,1,1024]{2,1,0:T(1,128)S(1)} all-to-all(f32[8,1,1024]{2,1,0:T(1,128)S(1)} %reshape.315), channel_id=1, replica_groups=mesh['gx'=8,'gz'=4] {'gx'}, dimensions={0} | all-to-all | bytes 65536 | tf_op jit(solution)/shard_map/all_to_all | solution.py:131
  51.8 0.5 broadcast.366
  52.3 0.7 %reduce.38 = f32[8,1024]{1,0:T(8,128)S(1)} reduce(f32[8,1,1024]{2,1,0:T(1,128)S(1)} %all_to_all.33, f32[]{:T(128)} %broadcast.366), dimensions={1}, to_apply=%all_to_all.24.reduce_sub_computation | reduce | bytes 65540 | tf_op jit(solution)/shard_map/all_to_all | solution.py:131
  53.4 0.3 fusion.20
  53.8 0.3 convolution_bitcast_fusion
  54.1 0.5 copy.226
  54.8 6.5 %all_to_all.34 = f32[4,1,4096]{2,1,0:T(1,128)S(1)} all-to-all(f32[4,1,4096]{2,1,0:T(1,128)S(1)} %reshape.317), channel_id=1, replica_groups=mesh['gx'=8,'gz'=4] {'gz'}, dimensions={0} | all-to-all | bytes 131072 | tf_op jit(solution)/shard_map/all_to_all | solution.py:136
  61.3 0.8 %reduce.39 = f32[4,4096]{1,0:T(4,128)S(1)} reduce(f32[4,1,4096]{2,1,0:T(1,128)S(1)} %all_to_all.34, f32[]{:T(128)} %broadcast.366), dimensions={1}, to_apply=%all_to_all.28.reduce_sub_computation | reduce | bytes 131076 | tf_op jit(solution)/shard_map/all_to_all | solution.py:136
  63.0 0.3 fusion.154
  63.5 0.3 fusion.156
  63.9 0.3 fusion.21
  64.2 0.3 fusion.22
  64.6 0.7 %copy.230 = f32[2,16,8,64]{3,2,1,0:T(8,128)} copy(f32[2,16,8,64]{3,1,2,0:T(8,128)S(1)} %pad_maximum_fusion.15) | data formatting | bytes 131072 | tf_op jit(solution)/shard_map/stack | solution.py:146
  (87 shorter events, 6.8 us)
Async XLA Ops:
  0.0 2.9 %copy-start.1 = (f32[19,4,16,128]{3,2,1,0:T(8,128)S(1)}, f32[19,4,16,128]{3,2,1,0:T(8,128)}, u32[]{:S(2)}) copy-start(f32[19,4,16,128]{3,2,1,0:T(8,128)} %param.11) | copy-start | bytes 1867780
  4.2 9.5 %collective-permute-start.1 = (f32[20,1,16,128]{3,2,1,0:T(8,128)S(1)}, f32[20,1,16,128]{3,2,1,0:T(8,128)S(1)}, u32[]{:S(2)}, u32[]{:S(2)}) collective-permute-start(f32[20,1,16,128]{3,2,1,0:T(8,128)S(1)} %get-tuple-element.64), channel_id=1, source_target_pairs={{4,0},{8,4},{12,8},{16,12},{20,16},{24,20},{28,24},{0,28},{5,1},{9... | collective-permute-start | bytes 491528 | tf_op jit(solution)/shard_map/ppermute | solution.py:45
  10.3 8.4 %collective-permute-start = (f32[20,1,16,128]{3,2,1,0:T(8,128)S(1)}, f32[20,1,16,128]{3,2,1,0:T(8,128)S(1)}, u32[]{:S(2)}, u32[]{:S(2)}) collective-permute-start(f32[20,1,16,128]{3,2,1,0:T(8,128)S(1)} %get-tuple-element.65), channel_id=1, source_target_pairs={{0,4},{4,8},{8,12},{12,16},{16,20},{20,24},{24,28},{28,0},{1,5},{5... | collective-permute-start | bytes 491528 | tf_op jit(solution)/shard_map/ppermute | solution.py:43
  18.7 0.8 %copy-start = (s32[4,16,128]{2,1,0:T(8,128)S(1)}, s32[4,16,128]{2,1,0:T(8,128)}, u32[]{:S(2)}) copy-start(s32[4,16,128]{2,1,0:T(8,128)} %param.12) | copy-start | bytes 98308
  18.8 1.9 %collective-permute-start.3 = (f32[20,6,1,128]{3,2,1,0:T(1,128)S(1)}, f32[20,6,1,128]{3,2,1,0:T(1,128)S(1)}, u32[]{:S(2)}, u32[]{:S(2)}) collective-permute-start(f32[20,6,1,128]{3,2,1,0:T(1,128)S(1)} %get-tuple-element.57), channel_id=1, source_target_pairs={{1,0},{2,1},{3,2},{0,3},{5,4},{6,5},{7,6},{4,7},{9,8},{10,9},{11,1... | collective-permute-start | bytes 184328 | tf_op jit(solution)/shard_map/ppermute | solution.py:45
  18.9 4.3 %collective-permute-start.2 = (f32[20,6,1,128]{3,2,1,0:T(1,128)S(1)}, f32[20,6,1,128]{3,2,1,0:T(1,128)S(1)}, u32[]{:S(2)}, u32[]{:S(2)}) collective-permute-start(f32[20,6,1,128]{3,2,1,0:T(1,128)S(1)} %get-tuple-element.56), channel_id=1, source_target_pairs={{0,1},{1,2},{2,3},{3,0},{4,5},{5,6},{6,7},{7,4},{8,9},{9,10},{10,1... | collective-permute-start | bytes 184328 | tf_op jit(solution)/shard_map/ppermute | solution.py:43
  24.6 0.7 %copy-start.2 = (f32[19]{0:T(128)S(1)}, f32[19]{0:T(128)}, u32[]{:S(2)}) copy-start(f32[19]{0:T(128)} %constant.62.clone) | copy-start | bytes 232
  24.6 0.7 %copy-start.3 = (f32[19]{0:T(128)S(1)}, f32[19]{0:T(128)}, u32[]{:S(2)}) copy-start(f32[19]{0:T(128)} %constant.63.clone) | copy-start | bytes 232
  24.6 0.7 %copy-start.4 = (f32[19]{0:T(128)S(1)}, f32[19]{0:T(128)}, u32[]{:S(2)}) copy-start(f32[19]{0:T(128)} %constant.64.clone) | copy-start | bytes 232
  25.3 0.7 %copy-start.5 = (f32[19]{0:T(128)S(1)}, f32[19]{0:T(128)}, u32[]{:S(2)}) copy-start(f32[19]{0:T(128)} %constant.73) | copy-start | bytes 232
  25.3 0.7 %copy-start.6 = (f32[19]{0:T(128)S(1)}, f32[19]{0:T(128)}, u32[]{:S(2)}) copy-start(f32[19]{0:T(128)} %constant.65.clone) | copy-start | bytes 232
  26.5 6.3 %collective-permute-start.5 = (f32[20,1,16,128]{3,2,1,0:T(8,128)S(1)}, f32[20,1,16,128]{3,2,1,0:T(8,128)S(1)}, u32[]{:S(2)}, u32[]{:S(2)}) collective-permute-start(f32[20,1,16,128]{3,2,1,0:T(8,128)S(1)} %get-tuple-element.60), channel_id=1, source_target_pairs={{4,0},{8,4},{12,8},{16,12},{20,16},{24,20},{28,24},{0,28},{5,1},{9... | collective-permute-start | bytes 491528 | tf_op jit(solution)/shard_map/ppermute | solution.py:45
  27.9 8.6 %collective-permute-start.4 = (f32[20,1,16,128]{3,2,1,0:T(8,128)S(1)}, f32[20,1,16,128]{3,2,1,0:T(8,128)S(1)}, u32[]{:S(2)}, u32[]{:S(2)}) collective-permute-start(f32[20,1,16,128]{3,2,1,0:T(8,128)S(1)} %get-tuple-element.61), channel_id=1, source_target_pairs={{0,4},{4,8},{8,12},{12,16},{16,20},{20,24},{24,28},{28,0},{1,5},{5... | collective-permute-start | bytes 491528 | tf_op jit(solution)/shard_map/ppermute | solution.py:43
  36.7 2.5 %collective-permute-start.7 = (f32[20,6,1,128]{3,2,1,0:T(1,128)S(1)}, f32[20,6,1,128]{3,2,1,0:T(1,128)S(1)}, u32[]{:S(2)}, u32[]{:S(2)}) collective-permute-start(f32[20,6,1,128]{3,2,1,0:T(1,128)S(1)} %get-tuple-element.53), channel_id=1, source_target_pairs={{1,0},{2,1},{3,2},{0,3},{5,4},{6,5},{7,6},{4,7},{9,8},{10,9},{11,1... | collective-permute-start | bytes 184328 | tf_op jit(solution)/shard_map/ppermute | solution.py:45
  36.7 3.7 %collective-permute-start.6 = (f32[20,6,1,128]{3,2,1,0:T(1,128)S(1)}, f32[20,6,1,128]{3,2,1,0:T(1,128)S(1)}, u32[]{:S(2)}, u32[]{:S(2)}) collective-permute-start(f32[20,6,1,128]{3,2,1,0:T(1,128)S(1)} %get-tuple-element.52), channel_id=1, source_target_pairs={{0,1},{1,2},{2,3},{3,0},{4,5},{5,6},{6,7},{7,4},{8,9},{9,10},{10,1... | collective-permute-start | bytes 184328 | tf_op jit(solution)/shard_map/ppermute | solution.py:43
where the time goes:
time: 65.6 us; the launch traced here: 65.3 us
  waiting for transfers between devices  23 us (35%)
  blocking collectives  15.5 us (24%)
  other arithmetic  10.4 us (16%)
  starting transfers between devices  9.25 us (14%)
  local copies, waits for them, and re-layouts  4.55 us (7%)
  matrix products  2 us (3%)
    ppermute x4, waiting for transfers between devices, with_halo(): lax.ppermute(tail, axis, [(i, (i + 1) % count) for i in range(count)])  12.4 us
    ppermute x4, waiting for transfers between devices, with_halo(): lax.ppermute(head, axis, [((i + 1) % count, i) for i in range(count)])  10.5 us
    all_to_all x1, blocking collectives, shards(): lax.all_to_all(columns, 'gx', split_axis=0, concat_axis=2, tiled=True)  9.06 us
    ppermute x4, starting transfers between devices, with_halo(): lax.ppermute(head, axis, [((i + 1) % count, i) for i in range(count)])  7.55 us
    all_to_all x1, blocking collectives, shards(): lax.all_to_all(along_kx, 'gz', split_axis=3, concat_axis=2, tiled=True)  6.49 us
    unnamed x34, other arithmetic  1.78 us
    select_n x2, other arithmetic, collide(): return jnp.where(fluid_cells > 0, relaxed, current)  1.71 us
    ppermute x4, starting transfers between devices, with_halo(): lax.ppermute(tail, axis, [(i, (i + 1) % count) for i in range(count)])  1.7 us
  transfers between devices with their start and end apart: 8, of which 8 were waited for; matrix products, arithmetic and copies ran while one was open for 0% of the time, Pallas kernels for 0%

commit v1 on v0

v1 whole, which is shorter than its diff:
```python
import functools
import math

import jax
import jax.numpy as jnp
import numpy as np
from jax import lax
from jax.experimental import pallas as pl
from jax.experimental.pallas import tpu as pltpu
from jax.sharding import PartitionSpec as P

VELOCITIES = (
    (0, 0, 0),
    (1, 0, 0),
    (-1, 0, 0),
    (0, 1, 0),
    (0, -1, 0),
    (0, 0, 1),
    (0, 0, -1),
    (1, 1, 0),
    (-1, -1, 0),
    (1, -1, 0),
    (-1, 1, 0),
    (1, 0, 1),
    (-1, 0, -1),
    (1, 0, -1),
    (-1, 0, 1),
    (0, 1, 1),
    (0, -1, -1),
    (0, 1, -1),
    (0, -1, 1),
)
LATTICE_WEIGHTS = (1.0 / 3.0,) + (1.0 / 18.0,) * 6 + (1.0 / 36.0,) * 12
OPPOSITES = (0, 2, 1, 4, 3, 6, 5, 8, 7, 10, 9, 12, 11, 14, 13, 16, 15, 18, 17)
RELAX_TIME = 0.6
BODY_FORCE = 0.0001
SPEED_UNIT = 0.05

CHAIN = (13, 1, 7, 9, 11, 5, 15, 18, 14, 2, 8, 10, 12, 6, 16, 17, 0, 3, 4)
SLOT = {number: CHAIN.index(number) for number in CHAIN}
X_FIRST = {1: 0, -1: 8}
Z_FIRST = {1: 4, -1: 12}
SIDES = ((1, 0), (-1, 0), (0, 1), (0, -1))
DIAGONALS = ((1, 1), (1, -1), (-1, 1), (-1, -1))
DIAGONAL_SLOT = (4, 0, 8, 12)
TOP = 8
MESH = pl.DeviceIdType.MESH


def collide(f, fluid):
    omega = 1.0 / RELAX_TIME
    keep = 1.0 - omega
    plus = {}
    minus = {}
    for i in range(1, 19, 2):
        plus[i] = f[i] + f[i + 1]
        minus[i] = f[i] - f[i + 1]
    density = f[0]
    momentum = [None, None, None]
    for i in range(1, 19, 2):
        density = density + plus[i]
        for axis in range(3):
            c = VELOCITIES[i][axis]
            if c:
                term = minus[i] if c > 0 else -minus[i]
                momentum[axis] = term if momentum[axis] is None else momentum[axis] + term
    inverse = 1.0 / density
    jx, jy, jz = momentum
    square = (jx * jx + jy * jy + jz * jz) * inverse
    base = density - 1.5 * square
    force = density * BODY_FORCE
    out = [None] * 19
    w0 = LATTICE_WEIGHTS[0] * omega
    out[0] = jnp.where(fluid, keep * f[0] + w0 * base, f[0])
    for i in range(1, 19, 2):
        w = LATTICE_WEIGHTS[i]
        cj = None
        for axis in range(3):
            c = VELOCITIES[i][axis]
            if c:
                j = momentum[axis]
                if cj is None:
                    cj = j if c > 0 else -j
                else:
                    cj = cj + j if c > 0 else cj - j
        even = (w * omega) * (base + 4.5 * (cj * cj * inverse))
        odd = (3.0 * w * omega) * cj
        if VELOCITIES[i][0]:
            odd = odd + (3.0 * w * VELOCITIES[i][0]) * force
        out[i] = jnp.where(fluid, keep * f[i] + (even + odd), f[i])
        out[i + 1] = jnp.where(fluid, keep * f[i + 1] + (even - odd), f[i + 1])
    return out


def tables(count_x, count_z, extent_x, extent_z, norm):
    lane = np.arange(128)
    step = (lane // extent_z) % extent_x
    k0 = np.arange(8)[:, None]
    angle = 2.0 * np.pi * k0 * step[None, :] / (count_x * extent_x)
    twiddle = np.concatenate([np.cos(angle), np.sin(angle)], axis=0)
    quarter_cos = np.array([1.0, 0.0, -1.0, 0.0])
    quarter_sin = np.array([0.0, 1.0, 0.0, -1.0])
    k1 = np.arange(4)[:, None]
    xl = np.arange(4)[None, :]
    c = quarter_cos[(k1 * xl) % 4]
    s = quarter_sin[(k1 * xl) % 4]
    block = np.zeros((4, 2, 2, 4))
    block[:, 0, 0] = c
    block[:, 0, 1] = s
    block[:, 1, 1] = c
    block[:, 1, 0] = -s
    first = np.einsum("kpqx,zw->kpzqxw", block, np.eye(extent_z)).reshape(128, 128)
    full_z = count_z * extent_z
    z = np.arange(full_z)
    angle = 2.0 * np.pi * ((z[:, None] * z[None, :]) % full_z) / full_z
    c = np.cos(angle) * norm
    s = np.sin(angle) * norm
    second = np.zeros((2, full_z, 2, full_z))
    second[0, :, 0] = c
    second[1, :, 0] = s
    second[1, :, 1] = c
    second[0, :, 1] = -s
    second = second.reshape(2, count_z, extent_z, 2, full_z).transpose(1, 0, 2, 3, 4)
    second = second.reshape(128, 128)
    return np.concatenate([twiddle, first, second], axis=0).astype(np.float32)


def halves(value):
    high = value.astype(jnp.bfloat16)
    low = (value - high.astype(jnp.float32)).astype(jnp.bfloat16)
    return high, low


def eight_point(v):
    r = math.sqrt(0.5)
    a0, a1, a2, a3 = v[0] + v[4], v[1] + v[5], v[2] + v[6], v[3] + v[7]
    b0, b1, b2, b3 = v[0] - v[4], v[1] - v[5], v[2] - v[6], v[3] - v[7]
    e0, e1 = a0 + a2, a1 + a3
    d, t = r * (b1 - b3), r * (b1 + b3)
    re = [e0 + e1, b0 + d, a0 - a2, b0 - d, e0 - e1]
    im = [None, -b2 - t, a3 - a1, b2 - t, None]
    re = re + [re[3], re[2], re[1]]
    im = im + [-im[3], -im[2], -im[1]]
    return re, im


def kernel(spectral, populations, fluid_mask, table, *rest):
    if spectral:
        (out_ref, held, mask_i, rolled, plain, walls, edges_out, edges_in, corners_out, corners_in,
         in_sem, halo_send, halo_recv, mask_send, mask_recv,
         ux, sent_x, got_x, left, sent_z, got_z, weights, table_sem, x_send, x_recv, z_send, z_recv) = rest
    else:
        (out_ref, held, mask_i, rolled, plain, walls, edges_out, edges_in, corners_out, corners_in,
         in_sem, halo_send, halo_recv, mask_send, mask_recv) = rest
    extent_x, extent_z, height = fluid_mask.shape
    count_x, count_z = lax.axis_size("gx"), lax.axis_size("gz")
    mx, mz = lax.axis_index("gx"), lax.axis_index("gz")

    def shifted_x(step):
        return lax.rem(mx + step + count_x, count_x)

    def shifted_z(step):
        return lax.rem(mz + step + count_z, count_z)

    inner = pl.ds(TOP, extent_z)

    mask_copy = pltpu.make_async_copy(fluid_mask, mask_i, in_sem.at[extent_x])
    mask_copy.start()
    fetches = []
    for x in range(extent_x):
        fetch = pltpu.make_async_copy(populations.at[:, x], held.at[x], in_sem.at[x])
        fetch.start()
        fetches.append(fetch)
    if spectral:
        table_copy = pltpu.make_async_copy(table, weights, table_sem.at[0])
        table_copy.start()

    barrier = pltpu.get_barrier_semaphore()
    partners = [(shifted_x(dx), shifted_z(dz)) for dx, dz in SIDES + DIAGONALS]
    if spectral:
        partners += [(shifted_x(p), mz) for p in range(2, count_x - 1)]
        partners += [(mx, shifted_z(p)) for p in range(2, count_z - 1)]
    for partner in partners:
        pl.semaphore_signal(barrier, inc=1, device_id=partner, device_id_type=MESH)

    lanes = lax.broadcasted_iota(jnp.int32, (extent_z, height), 1)

    def store(step, x, g):
        for number in range(19):
            cy = VELOCITIES[number][1]
            value = g[number]
            if cy:
                plain[number, x] = value
                value = pltpu.roll(value, cy % height, 1)
            slot = SLOT[number]
            rolled[step, slot, 1 + x, inner, :] = value
            cz = VELOCITIES[number][2]
            if cz:
                order = (slot - Z_FIRST[cz]) % 16
                row = extent_z - 1 if cz > 0 else 0
                edge = value[row : row + 1, :]
                side = 0 if cz > 0 else 1
                edges_out[step, side, pl.ds(order * extent_x + x, 1), :] = edge
                cx = VELOCITIES[number][0]
                if cx and x == (extent_x - 1 if cx > 0 else 0):
                    diagonal = DIAGONALS.index((cx, cz))
                    corners_out[step, diagonal, pl.ds(0, 1), :] = edge

    mask_copy.wait()
    fluids = []
    for x in range(extent_x):
        fetches[x].wait()
        solid = mask_i[x].astype(jnp.float32)
        walls[0, 1 + x, inner, :] = solid
        for step in range(2):
            for side in range(2):
                row = extent_z - 1 if side == 0 else 0
                edges_out[step, side, pl.ds(5 * extent_x + x, 1), :] = solid[row : row + 1, :]
            for diagonal, (cx, cz) in enumerate(DIAGONALS):
                if x == (extent_x - 1 if cx > 0 else 0):
                    row = extent_z - 1 if cz > 0 else 0
                    corners_out[step, diagonal, pl.ds(1, 1), :] = solid[row : row + 1, :]
        g = collide([held[x, number] for number in range(19)], solid > 0)
        store(0, x, g)

    pl.semaphore_wait(barrier, len(partners))

    def send(step):
        copies = []
        for side, (dx, dz) in enumerate(SIDES):
            if dx:
                here, there = (extent_x, 0) if dx > 0 else (1, extent_x + 1)
                group = pl.ds(X_FIRST[dx], 5)
                source = rolled.at[step, group, here, inner]
                target = rolled.at[step, group, there, inner]
            else:
                which = 0 if dz > 0 else 1
                source = edges_out.at[step, which]
                target = edges_in.at[step, which]
            copies.append((source, target, dx, dz, side))
        for diagonal, (dx, dz) in enumerate(DIAGONALS):
            copies.append((corners_out.at[step, diagonal], corners_in.at[step, diagonal], dx, dz, 4 + diagonal))
        started = []
        if step == 0:
            for side in range(2):
                dx = SIDES[side][0]
                here, there = (extent_x, 0) if dx > 0 else (1, extent_x + 1)
                copy = pltpu.make_async_remote_copy(
                    src_ref=walls.at[0, here, inner],
                    dst_ref=walls.at[0, there, inner],
                    send_sem=mask_send.at[side],
                    recv_sem=mask_recv.at[side],
                    device_id=(shifted_x(dx), mz),
                    device_id_type=MESH,
                )
                copy.start()
                started.append(copy)
        for source, target, dx, dz, number in copies:
            copy = pltpu.make_async_remote_copy(
                src_ref=source,
                dst_ref=target,
                send_sem=halo_send.at[step, number],
                recv_sem=halo_recv.at[step, number],
                device_id=(shifted_x(dx), shifted_z(dz)),
                device_id_type=MESH,
            )
            copy.start()
            started.append(copy)
        return started

    def receive(step, started):
        for copy in started:
            copy.wait_recv()
        for side in range(2):
            row = TOP - 1 if side == 0 else TOP + extent_z
            first = Z_FIRST[1 if side == 0 else -1]
            for x in range(extent_x):
                for order in range(5):
                    rolled[step, (first + order) % 16, 1 + x, pl.ds(row, 1), :] = edges_in[
                        step, side, pl.ds(order * extent_x + x, 1), :
                    ]
                if step == 0:
                    walls[0, 1 + x, pl.ds(row, 1), :] = edges_in[step, side, pl.ds(5 * extent_x + x, 1), :]
        for diagonal, (cx, cz) in enumerate(DIAGONALS):
            plane = 0 if cx > 0 else extent_x + 1
            row = TOP - 1 if cz > 0 else TOP + extent_z
            slot = DIAGONAL_SLOT[diagonal]
            rolled[step, slot, plane, pl.ds(row, 1), :] = corners_in[step, diagonal, pl.ds(0, 1), :]
            if step == 0:
                walls[0, plane, pl.ds(row, 1), :] = corners_in[step, diagonal, pl.ds(1, 1), :]

    def shift_walls():
        around = lax.broadcasted_iota(jnp.int32, (extent_z + 2 * TOP, height), 1)
        for plane in range(extent_x + 2):
            value = walls[0, plane]
            walls[1, plane] = jnp.where(around == 0, 0.0, pltpu.roll(value, 1, 1))
            walls[2, plane] = jnp.where(around == height - 1, 0.0, pltpu.roll(value, height - 1, 1))

    def streamed(step, x):
        fluid = walls[0, 1 + x, inner, :] > 0

        def own(number):
            if VELOCITIES[number][1]:
                return plain[number, x]
            return rolled[step, SLOT[number], 1 + x, inner, :]

        owned = [own(number) for number in range(19)]
        f = [owned[0]]
        for number in range(1, 19):
            cx, cy, cz = VELOCITIES[number]
            slot = SLOT[number]
            rows = pl.ds(TOP - cz, extent_z)
            source_fluid = walls[(0, 1, 2)[cy], 1 + x - cx, rows, :] > 0
            value = rolled[step, slot, 1 + x - cx, rows, :]
            arrived = jnp.where(source_fluid, value, owned[OPPOSITES[number]])
            f.append(jnp.where(fluid, arrived, owned[number]))
        return f, fluid

    started = send(0)
    receive(0, started)
    shift_walls()
    for x in range(extent_x):
        f, fluid = streamed(0, x)
        g = collide(f, fluid)
        store(1, x, g)
    finish = started
    started = send(1)
    receive(1, started)
    for x in range(extent_x):
        f, fluid = streamed(1, x)
        density = f[0]
        forward = None
        for i in range(1, 19, 2):
            density = density + (f[i] + f[i + 1])
            c = VELOCITIES[i][0]
            if c:
                term = (f[i] - f[i + 1])
                forward = term if forward is None else forward + term
        speed = walls[0, 1 + x, inner, :] * forward / density
        if spectral:
            ux[pl.ds(x * extent_z, extent_z), :] = speed
        else:
            out_ref[x] = speed

    if spectral:
        whole = ux[...]
        both = jnp.concatenate([whole, pltpu.roll(whole, height - 8, 1)], axis=0)
        turned = both.T
        for a in range(count_x):
            sent_x[a] = turned[16 * a : 16 * a + 8, :]
        x_copies = []
        for p in range(1, count_x):
            there = shifted_x(p)
            copy = pltpu.make_async_remote_copy(
                src_ref=sent_x.at[there],
                dst_ref=got_x.at[mx],
                send_sem=x_send.at[p],
                recv_sem=x_recv.at[p],
                device_id=(there, mz),
                device_id_type=MESH,
            )
            copy.start()
            x_copies.append(copy)
        got_x[mx] = sent_x[mx]
        table_copy.wait()
        for copy in x_copies:
            copy.wait_recv()
        re, im = eight_point([got_x[s] for s in range(8)])
        low_lanes = lax.broadcasted_iota(jnp.int32, (8, 128), 1) < 64
        for k in range(8):
            c = weights[pl.ds(k, 1), :]
            s = weights[pl.ds(8 + k, 1), :]
            if im[k] is None:
                real, imag = re[k] * c, -re[k] * s
            else:
                real, imag = re[k] * c + im[k] * s, im[k] * c - re[k] * s
            left[pl.ds(k, 8, stride=8), :] = jnp.where(low_lanes, real, pltpu.roll(imag, 64, 1))
            left[pl.ds(64 + k, 8, stride=8), :] = jnp.where(low_lanes, pltpu.roll(real, 64, 1), imag)
        high, low = halves(left[...])
        first = weights[pl.ds(16, 128), :].astype(jnp.bfloat16)
        contract = (((1,), (1,)), ((), ()))
        along = lax.dot_general(
            jnp.concatenate([first, first], axis=1),
            jnp.concatenate([high, low], axis=1),
            contract,
            preferred_element_type=jnp.float32,
        )
        for b in range(count_z):
            sent_z[b] = along[32 * b : 32 * b + 32, :]
        z_copies = []
        for p in range(1, count_z):
            there = shifted_z(p)
            copy = pltpu.make_async_remote_copy(
                src_ref=sent_z.at[there],
                dst_ref=got_z.at[mz],
                send_sem=z_send.at[p],
                recv_sem=z_recv.at[p],
                device_id=(mx, there),
                device_id_type=MESH,
            )
            copy.start()
            z_copies.append(copy)
        got_z[mz] = sent_z[mz]
        second_high, second_low = halves(weights[pl.ds(144, 128), :])
        second_twice = jnp.concatenate([second_high, second_high], axis=0)
        for copy in z_copies:
            copy.wait_recv()
        lines = got_z[...].reshape(128, 128).T
        high, low = halves(lines)
        result = jnp.dot(
            jnp.concatenate([high, low], axis=1), second_twice, preferred_element_type=jnp.float32
        ) + jnp.dot(high, second_low, preferred_element_type=jnp.float32)
        out_ref[0] = result[:, :64].reshape(16, 8, 64)
        out_ref[1] = result[:, 64:].reshape(16, 8, 64)
        for copy in x_copies + z_copies:
            copy.wait_send()
    for copy in finish + started:
        copy.wait_send()


def shards(populations, fluid_mask):
    number, extent_x, extent_z, height = populations.shape
    count_x, count_z = lax.axis_size("gx"), lax.axis_size("gz")
    full_x, full_z = count_x * extent_x, count_z * extent_z
    norm_scale = 1.0 / (math.sqrt(full_x * full_z) * SPEED_UNIT)
    spectral = (count_x, count_z, extent_x, extent_z, height) == (8, 4, 4, 16, 128)
    if spectral:
        table = jnp.asarray(tables(count_x, count_z, extent_x, extent_z, norm_scale))
    else:
        table = jnp.zeros((8, 128), jnp.float32)
    f32 = jnp.float32
    padded = (extent_x + 2, extent_z + 2 * TOP, height)
    edge_rows = 6 * extent_x
    dma = pltpu.SemaphoreType.DMA
    scratch = [
        pltpu.VMEM((extent_x, 19, extent_z, height), f32),
        pltpu.VMEM((extent_x, extent_z, height), jnp.int32),
        pltpu.VMEM((2, 19) + padded, f32),
        pltpu.VMEM((19, extent_x, extent_z, height), f32),
        pltpu.VMEM((3,) + padded, f32),
        pltpu.VMEM((2, 2, edge_rows, height), f32),
        pltpu.VMEM((2, 2, edge_rows, height), f32),
        pltpu.VMEM((2, 4, 2, height), f32),
        pltpu.VMEM((2, 4, 2, height), f32),
        dma((extent_x + 1,)),
        dma((2, 8)),
        dma((2, 8)),
        dma((2,)),
        dma((2,)),
    ]
    if spectral:
        scratch += [
            pltpu.VMEM((64, 128), f32),
            pltpu.VMEM((8, 8, 128), f32),
            pltpu.VMEM((8, 8, 128), f32),
            pltpu.VMEM((128, 128), f32),
            pltpu.VMEM((4, 32, 128), f32),
            pltpu.VMEM((4, 32, 128), f32),
            pltpu.VMEM(table.shape, f32),
            dma((1,)),
            dma((8,)),
            dma((8,)),
            dma((4,)),
            dma((4,)),
        ]
        out_shape = jax.ShapeDtypeStruct((2, 16, 8, 64), f32)
    else:
        out_shape = jax.ShapeDtypeStruct((extent_x, extent_z, height), f32)
    anywhere = pl.BlockSpec(memory_space=pl.ANY)
    result = pl.pallas_call(
        functools.partial(kernel, spectral),
        out_shape=out_shape,
        in_specs=[anywhere] * 3,
        out_specs=pl.BlockSpec(memory_space=pltpu.VMEM),
        scratch_shapes=scratch,
        compiler_params=pltpu.CompilerParams(
            collective_id=0, has_side_effects=True, vmem_limit_bytes=32 * 1024 * 1024
        ),
    )(populations, fluid_mask, table)
    if spectral:
        return result
    return spectrum(result, norm_scale)


def dft_tables(length, factor):
    index = jnp.arange(length, dtype=jnp.int32)
    products = index[:, None] * index[None, :] % length
    angles = products.astype(jnp.float32) * (2.0 * math.pi / length)
    return (jnp.cos(angles) * factor, jnp.sin(angles) * factor)


def spectrum(speed_x, norm_scale):
    columns = jnp.transpose(speed_x, (2, 1, 0))
    highest = lax.Precision.HIGHEST
    block = lax.all_to_all(columns, "gx", split_axis=0, concat_axis=2, tiled=True)
    cosine, sine = dft_tables(block.shape[2], norm_scale)
    real_part = jnp.einsum("yzx,xk->yzk", block, cosine, precision=highest)
    imag_part = -jnp.einsum("yzx,xk->yzk", block, sine, precision=highest)
    along_kx = jnp.stack([real_part, imag_part], axis=0)
    block = lax.all_to_all(along_kx, "gz", split_axis=3, concat_axis=2, tiled=True)
    cosine, sine = dft_tables(block.shape[2], 1.0)
    real_in = block[0]
    imag_in = block[1]
    real_part = jnp.einsum("ync,nk->yck", real_in, cosine, precision=highest) + jnp.einsum(
        "ync,nk->yck", imag_in, sine, precision=highest
    )
    imag_part = jnp.einsum("ync,nk->yck", imag_in, cosine, precision=highest) - jnp.einsum(
        "ync,nk->yck", real_in, sine, precision=highest
    )
    return jnp.stack([real_part, imag_part], axis=0)


def solution(mesh):
    placed = (P(None, "gx", "gz", None), P("gx", "gz", None))
    return jax.shard_map(
        shards, mesh=mesh, in_specs=placed, out_specs=P(None, "gx", "gz", None), check_vma=False
    )
```

time: 65.6 us -> 26.9 us (0.41)
  Pallas kernels: 0 us -> 23.3 us
  waiting for transfers between devices: 23 us -> 0 us
  blocking collectives: 15.5 us -> 0 us
  other arithmetic: 10.4 us -> 0 us
  starting transfers between devices: 9.25 us -> 0 us
  matrix products: 2 us -> 0 us
  local copies, waits for them, and re-layouts: 4.55 us -> 3.4 us
    pallas_call x0 -> x1, Pallas kernels: none -> 23.3 us  [shards(): pl.pallas_call(functools.partial(kernel, spectral), out_shape=out_shape,...]
    ppermute x8 -> x0, waiting for transfers between devices: 23 us -> none  [the longest x4 12.4 us: with_halo(): lax.ppermute(tail, axis, [(i, (i + 1) % count) for i in range(count)])]
    all_to_all x2 -> x0, blocking collectives: 15.5 us -> none  [the longest x1 9.06 us: shards(): lax.all_to_all(columns, 'gx', split_axis=0, concat_axis=2, tiled=True)]
    ppermute x8 -> x0, starting transfers between devices: 9.25 us -> none  [the longest x4 7.55 us: with_halo(): lax.ppermute(head, axis, [((i + 1) % count, i) for i in range(count)])]
    dot_general x6 -> x0, matrix products: 2 us -> none  [the longest x1 0.34 us: shards(): jnp.einsum('ync,nk->yck', imag_in, sine, precision=highest)]
    unnamed x20 -> x7, local copies, waits for them, and re-layouts: 1.56 us -> 3.4 us
    unnamed x34 -> x0, other arithmetic: 1.78 us -> none
    select_n x2 -> x0, other arithmetic: 1.71 us -> none  [collide(): return jnp.where(fluid_cells > 0, relaxed, current)]
  transfers between devices with their start and end apart: 8 -> 0, of which waited for: 8 -> 0; matrix products, arithmetic and copies ran while one was open for 0% -> 0% of each run, Pallas kernels for 0% -> 0%
where the time goes in v1:
time: 26.9 us; the launch traced here: 26.7 us
  Pallas kernels  23.3 us (87%)
  local copies, waits for them, and re-layouts  3.4 us (13%)
    pallas_call x1, Pallas kernels, shards(): pl.pallas_call(functools.partial(kernel, spectral), out_shape=out_shape,...  23.3 us
    unnamed x7, local copies, waits for them, and re-layouts  3.4 us

profile of v1, /device:TPU:0, one launch (start us, length us, event | category | flops | bytes accessed | tf_op | source)
XLA Modules:
  0.0 26.7 jit_solution(1017664296059227761)
XLA Ops:
  0.0 0.0 copy-start
  0.0 1.1 %copy-done = f32[19,4,16,128]{3,2,1,0:T(8,128)S(1)} copy-done((f32[19,4,16,128]{3,2,1,0:T(8,128)S(1)}, f32[19,4,16,128]{3,2,1,0:T(8,128)}, u32[]{:S(2)}) %copy-start) | copy-done | bytes 622616
  1.1 0.0 copy-start.1
  1.1 0.9 %copy-done.1 = f32[272,128]{1,0:T(8,128)S(1)} copy-done((f32[272,128]{1,0:T(8,128)S(1)}, f32[272,128]{1,0:T(8,128)}, u32[]{:S(2)}) %copy-start.1) | copy-done | bytes 139288
  2.0 0.0 copy-start.2
  2.0 0.8 %copy-done.2 = s32[4,16,128]{2,1,0:T(8,128)S(1)} copy-done((s32[4,16,128]{2,1,0:T(8,128)S(1)}, s32[4,16,128]{2,1,0:T(8,128)}, u32[]{:S(2)}) %copy-start.2) | copy-done | bytes 32792
  2.7 23.3 %shard_map.37 = f32[2,16,8,64]{3,2,1,0:T(8,128)S(1)} custom-call(f32[19,4,16,128]{3,2,1,0:T(8,128)S(1)} %copy-done, s32[4,16,128]{2,1,0:T(8,128)S(1)} %copy-done.2, f32[272,128]{1,0:T(8,128)S(1)} %copy-done.1), custom_call_target="tpu_custom_call" | custom-call | tf_op jit(solution)/shard_map/pallas_call | solution.py:470
  26.0 0.7 %copy.5 = f32[2,16,8,64]{3,2,1,0:T(8,128)} copy(f32[2,16,8,64]{3,2,1,0:T(8,128)S(1)} %shard_map.37) | data formatting | bytes 131072
Async XLA Ops:
  0.0 1.1 %copy-start = (f32[19,4,16,128]{3,2,1,0:T(8,128)S(1)}, f32[19,4,16,128]{3,2,1,0:T(8,128)}, u32[]{:S(2)}) copy-start(f32[19,4,16,128]{3,2,1,0:T(8,128)} %populations.1) | copy-start | bytes 1867780
  1.1 0.9 %copy-start.1 = (f32[272,128]{1,0:T(8,128)S(1)}, f32[272,128]{1,0:T(8,128)}, u32[]{:S(2)}) copy-start(f32[272,128]{1,0:T(8,128)} %constant.2.clone.table) | copy-start | bytes 417796
  2.0 0.8 %copy-start.2 = (s32[4,16,128]{2,1,0:T(8,128)S(1)}, s32[4,16,128]{2,1,0:T(8,128)}, u32[]{:S(2)}) copy-start(s32[4,16,128]{2,1,0:T(8,128)} %fluid_mask.1) | copy-start | bytes 98308

commit v2 on v1

--- a/solution.py
+++ b/solution.py
@@ -145,14 +145,14 @@
 
 
 def kernel(spectral, populations, fluid_mask, table, *rest):
-    if spectral:
-        (out_ref, held, mask_i, rolled, plain, walls, edges_out, edges_in, corners_out, corners_in,
-         in_sem, halo_send, halo_recv, mask_send, mask_recv,
-         ux, sent_x, got_x, left, sent_z, got_z, weights, table_sem, x_send, x_recv, z_send, z_recv) = rest
-    else:
-        (out_ref, held, mask_i, rolled, plain, walls, edges_out, edges_in, corners_out, corners_in,
-         in_sem, halo_send, halo_recv, mask_send, mask_recv) = rest
+    (out_ref, held, mask_i, rolled, plain, walls, edges_out, edges_in, corners_out, corners_in,
+     sums_in, rims_out, rims_in, tips_out, tips_in, density, forward, ahead, behind,
+     in_sem, halo_send, halo_recv, mask_send, mask_recv) = rest[:24]
+    if spectral:
+        (ux, sent_x, got_x, left, sent_z, got_z, weights,
+         table_sem, x_send, x_recv, z_send, z_recv) = rest[24:]
     extent_x, extent_z, height = fluid_mask.shape
+    last = extent_x - 1
     count_x, count_z = lax.axis_size("gx"), lax.axis_size("gz")
     mx, mz = lax.axis_index("gx"), lax.axis_index("gz")
 
@@ -163,17 +163,15 @@
         return lax.rem(mz + step + count_z, count_z)
 
     inner = pl.ds(TOP, extent_z)
+    outer_rows = (0, last)
+    inner_rows = tuple(range(1, last))
 
     mask_copy = pltpu.make_async_copy(fluid_mask, mask_i, in_sem.at[extent_x])
     mask_copy.start()
-    fetches = []
-    for x in range(extent_x):
-        fetch = pltpu.make_async_copy(populations.at[:, x], held.at[x], in_sem.at[x])
-        fetch.start()
-        fetches.append(fetch)
-    if spectral:
-        table_copy = pltpu.make_async_copy(table, weights, table_sem.at[0])
-        table_copy.start()
+    fetches = {}
+    for x in outer_rows + inner_rows:
+        fetches[x] = pltpu.make_async_copy(populations.at[:, x], held.at[x], in_sem.at[x])
+        fetches[x].start()
 
     barrier = pltpu.get_barrier_semaphore()
     partners = [(shifted_x(dx), shifted_z(dz)) for dx, dz in SIDES + DIAGONALS]
@@ -182,161 +180,228 @@
         partners += [(mx, shifted_z(p)) for p in range(2, count_z - 1)]
     for partner in partners:
         pl.semaphore_signal(barrier, inc=1, device_id=partner, device_id_type=MESH)
+    if spectral:
+        table_copy = pltpu.make_async_copy(table, weights, table_sem.at[0])
+        table_copy.start()
 
     lanes = lax.broadcasted_iota(jnp.int32, (extent_z, height), 1)
-
-    def store(step, x, g):
+    rows = lax.broadcasted_iota(jnp.int32, (extent_z, height), 0)
+
+    def edge_of(value, cz):
+        row = extent_z - 1 if cz > 0 else 0
+        return value[row : row + 1, :]
+
+    def first_collision(x):
+        fetches[x].wait()
+        solid = mask_i[x].astype(jnp.float32)
+        walls[0, 1 + x, inner, :] = solid
+        for side, cz in enumerate((1, -1)):
+            edges_out[side, pl.ds(5 * extent_x + x, 1), :] = edge_of(solid, cz)
+        for diagonal, (cx, cz) in enumerate(DIAGONALS):
+            if x == (last if cx > 0 else 0):
+                corners_out[diagonal, pl.ds(1, 1), :] = edge_of(solid, cz)
+        g = collide([held[x, number] for number in range(19)], solid > 0)
         for number in range(19):
-            cy = VELOCITIES[number][1]
+            cx, cy, cz = VELOCITIES[number]
             value = g[number]
             if cy:
                 plain[number, x] = value
                 value = pltpu.roll(value, cy % height, 1)
             slot = SLOT[number]
-            rolled[step, slot, 1 + x, inner, :] = value
-            cz = VELOCITIES[number][2]
+            rolled[slot, 1 + x, inner, :] = value
             if cz:
                 order = (slot - Z_FIRST[cz]) % 16
-                row = extent_z - 1 if cz > 0 else 0
-                edge = value[row : row + 1, :]
-                side = 0 if cz > 0 else 1
-                edges_out[step, side, pl.ds(order * extent_x + x, 1), :] = edge
-                cx = VELOCITIES[number][0]
-                if cx and x == (extent_x - 1 if cx > 0 else 0):
-                    diagonal = DIAGONALS.index((cx, cz))
-                    corners_out[step, diagonal, pl.ds(0, 1), :] = edge
+                edge = edge_of(value, cz)
+                edges_out[0 if cz > 0 else 1, pl.ds(order * extent_x + x, 1), :] = edge
+                if cx and x == (last if cx > 0 else 0):
+                    corners_out[DIAGONALS.index((cx, cz)), pl.ds(0, 1), :] = edge
+
+    def send(source, target, send_sem, recv_sem, dx, dz):
+        copy = pltpu.make_async_remote_copy(
+            src_ref=source,
+            dst_ref=target,
+            send_sem=send_sem,
+            recv_sem=recv_sem,
+            device_id=(shifted_x(dx), shifted_z(dz)),
+            device_id_type=MESH,
+        )
+        copy.start()
+        return copy
 
     mask_copy.wait()
-    fluids = []
-    for x in range(extent_x):
-        fetches[x].wait()
-        solid = mask_i[x].astype(jnp.float32)
-        walls[0, 1 + x, inner, :] = solid
-        for step in range(2):
-            for side in range(2):
-                row = extent_z - 1 if side == 0 else 0
-                edges_out[step, side, pl.ds(5 * extent_x + x, 1), :] = solid[row : row + 1, :]
-            for diagonal, (cx, cz) in enumerate(DIAGONALS):
-                if x == (extent_x - 1 if cx > 0 else 0):
-                    row = extent_z - 1 if cz > 0 else 0
-                    corners_out[step, diagonal, pl.ds(1, 1), :] = solid[row : row + 1, :]
-        g = collide([held[x, number] for number in range(19)], solid > 0)
-        store(0, x, g)
-
+    for x in outer_rows:
+        first_collision(x)
     pl.semaphore_wait(barrier, len(partners))
-
-    def send(step):
-        copies = []
-        for side, (dx, dz) in enumerate(SIDES):
-            if dx:
-                here, there = (extent_x, 0) if dx > 0 else (1, extent_x + 1)
-                group = pl.ds(X_FIRST[dx], 5)
-                source = rolled.at[step, group, here, inner]
-                target = rolled.at[step, group, there, inner]
+    x_sides, z_sides, corners = [], [], []
+    for side, dx in enumerate((1, -1)):
+        here, there = (extent_x, 0) if dx > 0 else (1, extent_x + 1)
+        group = pl.ds(X_FIRST[dx], 5)
+        x_sides.append(
+            send(rolled.at[group, here, inner], rolled.at[group, there, inner],
+                 halo_send.at[0, side], halo_recv.at[0, side], dx, 0)
+        )
+        x_sides.append(
+            send(walls.at[0, here, inner], walls.at[0, there, inner],
+                 mask_send.at[side], mask_recv.at[side], dx, 0)
+        )
+    for x in inner_rows:
+        first_collision(x)
+    for side, dz in enumerate((1, -1)):
+        z_sides.append(
+            send(edges_out.at[side], edges_in.at[side],
+                 halo_send.at[0, 2 + side], halo_recv.at[0, 2 + side], 0, dz)
+        )
+    for diagonal, (dx, dz) in enumerate(DIAGONALS):
+        corners.append(
+            send(corners_out.at[diagonal], corners_in.at[diagonal],
+                 halo_send.at[0, 4 + diagonal], halo_recv.at[0, 4 + diagonal], dx, dz)
+        )
+
+    around = lax.broadcasted_iota(jnp.int32, (extent_z + 2 * TOP, height), 1)
+
+    def shift_walls(plane):
+        value = walls[0, plane]
+        walls[1, plane] = jnp.where(around == 0, 0.0, pltpu.roll(value, 1, 1))
+        walls[2, plane] = jnp.where(around == height - 1, 0.0, pltpu.roll(value, height - 1, 1))
+
+    def wall_from(number, x):
+        cx, cy, cz = VELOCITIES[number]
+        return walls[(0, 1, 2)[cy], 1 + x - cx, pl.ds(TOP - cz, extent_z), :] > 0
+
+    def streamed(x, fluid):
+        owned = []
+        for number in range(19):
+            if VELOCITIES[number][1]:
+                owned.append(plain[number, x])
             else:
-                which = 0 if dz > 0 else 1
-                source = edges_out.at[step, which]
-                target = edges_in.at[step, which]
-            copies.append((source, target, dx, dz, side))
-        for diagonal, (dx, dz) in enumerate(DIAGONALS):
-            copies.append((corners_out.at[step, diagonal], corners_in.at[step, diagonal], dx, dz, 4 + diagonal))
-        started = []
-        if step == 0:
-            for side in range(2):
-                dx = SIDES[side][0]
-                here, there = (extent_x, 0) if dx > 0 else (1, extent_x + 1)
-                copy = pltpu.make_async_remote_copy(
-                    src_ref=walls.at[0, here, inner],
-                    dst_ref=walls.at[0, there, inner],
-                    send_sem=mask_send.at[side],
-                    recv_sem=mask_recv.at[side],
-                    device_id=(shifted_x(dx), mz),
-                    device_id_type=MESH,
-                )
-                copy.start()
-                started.append(copy)
-        for source, target, dx, dz, number in copies:
-            copy = pltpu.make_async_remote_copy(
-                src_ref=source,
-                dst_ref=target,
-                send_sem=halo_send.at[step, number],
-                recv_sem=halo_recv.at[step, number],
-                device_id=(shifted_x(dx), shifted_z(dz)),
-                device_id_type=MESH,
-            )
-            copy.start()
-            started.append(copy)
-        return started
-
-    def receive(step, started):
-        for copy in started:
-            copy.wait_recv()
-        for side in range(2):
-            row = TOP - 1 if side == 0 else TOP + extent_z
-            first = Z_FIRST[1 if side == 0 else -1]
-            for x in range(extent_x):
-                for order in range(5):
-                    rolled[step, (first + order) % 16, 1 + x, pl.ds(row, 1), :] = edges_in[
-                        step, side, pl.ds(order * extent_x + x, 1), :
-                    ]
-                if step == 0:
-                    walls[0, 1 + x, pl.ds(row, 1), :] = edges_in[step, side, pl.ds(5 * extent_x + x, 1), :]
-        for diagonal, (cx, cz) in enumerate(DIAGONALS):
-            plane = 0 if cx > 0 else extent_x + 1
-            row = TOP - 1 if cz > 0 else TOP + extent_z
-            slot = DIAGONAL_SLOT[diagonal]
-            rolled[step, slot, plane, pl.ds(row, 1), :] = corners_in[step, diagonal, pl.ds(0, 1), :]
-            if step == 0:
-                walls[0, plane, pl.ds(row, 1), :] = corners_in[step, diagonal, pl.ds(1, 1), :]
-
-    def shift_walls():
-        around = lax.broadcasted_iota(jnp.int32, (extent_z + 2 * TOP, height), 1)
-        for plane in range(extent_x + 2):
-            value = walls[0, plane]
-            walls[1, plane] = jnp.where(around == 0, 0.0, pltpu.roll(value, 1, 1))
-            walls[2, plane] = jnp.where(around == height - 1, 0.0, pltpu.roll(value, height - 1, 1))
-
-    def streamed(step, x):
-        fluid = walls[0, 1 + x, inner, :] > 0
-
-        def own(number):
-            if VELOCITIES[number][1]:
-                return plain[number, x]
-            return rolled[step, SLOT[number], 1 + x, inner, :]
-
-        owned = [own(number) for number in range(19)]
+                owned.append(rolled[SLOT[number], 1 + x, inner, :])
         f = [owned[0]]
         for number in range(1, 19):
             cx, cy, cz = VELOCITIES[number]
-            slot = SLOT[number]
-            rows = pl.ds(TOP - cz, extent_z)
-            source_fluid = walls[(0, 1, 2)[cy], 1 + x - cx, rows, :] > 0
-            value = rolled[step, slot, 1 + x - cx, rows, :]
-            arrived = jnp.where(source_fluid, value, owned[OPPOSITES[number]])
+            value = rolled[SLOT[number], 1 + x - cx, pl.ds(TOP - cz, extent_z), :]
+            arrived = jnp.where(wall_from(number, x), value, owned[OPPOSITES[number]])
             f.append(jnp.where(fluid, arrived, owned[number]))
-        return f, fluid
-
-    started = send(0)
-    receive(0, started)
-    shift_walls()
+        return f
+
+    rims = {}
+
+    def second_collision(x):
+        fluid = walls[0, 1 + x, inner, :] > 0
+        g = collide(streamed(x, fluid), fluid)
+        for number in range(19):
+            held[x, number] = g[number]
+        leaving = {}
+        for number in range(1, 19):
+            cx, cy, cz = VELOCITIES[number]
+            value = jnp.where(fluid, g[number], 0.0)
+            if cy:
+                value = pltpu.roll(value, cy % height, 1)
+                value = jnp.where(lanes == (0 if cy > 0 else height - 1), 0.0, value)
+            leaving[cx, cz] = leaving[cx, cz] + value if (cx, cz) in leaving else value
+        for cx, keep in ((1, ahead), (-1, behind), (0, None)):
+            total = leaving[cx, 0]
+            for cz in (1, -1):
+                value = leaving[cx, cz]
+                rims[x, cx, cz] = edge_of(value, cz)
+                moved = pltpu.roll(value, cz % extent_z, 0)
+                total = total + jnp.where(rows == (0 if cz > 0 else extent_z - 1), 0.0, moved)
+            if keep is None:
+                density[x] = g[0] + total
+            else:
+                keep[x] = total
+
+    def bounced(x):
+        sums = {}
+        for number in range(1, 19):
+            cx = VELOCITIES[number][0]
+            value = jnp.where(wall_from(number, x), 0.0, held[x, OPPOSITES[number]])
+            sums[cx] = sums[cx] + value if cx in sums else value
+        density[x] = density[x] + (sums[0] + sums[1] + sums[-1])
+        forward[x] = sums[1] - sums[-1]
+
+    for copy in z_sides:
+        copy.wait_recv()
+    for side, cz in enumerate((1, -1)):
+        row = TOP - 1 if cz > 0 else TOP + extent_z
+        for x in range(extent_x):
+            for order in range(5):
+                rolled[(Z_FIRST[cz] + order) % 16, 1 + x, pl.ds(row, 1), :] = edges_in[
+                    side, pl.ds(order * extent_x + x, 1), :
+                ]
+            walls[0, 1 + x, pl.ds(row, 1), :] = edges_in[side, pl.ds(5 * extent_x + x, 1), :]
     for x in range(extent_x):
-        f, fluid = streamed(0, x)
-        g = collide(f, fluid)
-        store(1, x, g)
-    finish = started
-    started = send(1)
-    receive(1, started)
+        shift_walls(1 + x)
+    for x in inner_rows:
+        second_collision(x)
+        bounced(x)
+    for copy in x_sides + corners:
+        copy.wait_recv()
+    for diagonal, (cx, cz) in enumerate(DIAGONALS):
+        plane = 0 if cx > 0 else extent_x + 1
+        row = TOP - 1 if cz > 0 else TOP + extent_z
+        rolled[DIAGONAL_SLOT[diagonal], plane, pl.ds(row, 1), :] = corners_in[diagonal, pl.ds(0, 1), :]
+        walls[0, plane, pl.ds(row, 1), :] = corners_in[diagonal, pl.ds(1, 1), :]
+    for plane in (0, extent_x + 1):
+        shift_walls(plane)
+    for x in outer_rows:
+        second_collision(x)
+
+    sums = []
+    for side, (dx, x, keep) in enumerate(((1, last, ahead), (-1, 0, behind))):
+        sums.append(
+            send(keep.at[x], sums_in.at[side],
+                 halo_send.at[1, side], halo_recv.at[1, side], dx, 0)
+        )
+    for side, dz in enumerate((1, -1)):
+        for x in range(extent_x):
+            total, along = rims[x, 0, dz], None
+            if x > 0:
+                total, along = total + rims[x - 1, 1, dz], rims[x - 1, 1, dz]
+            if x < last:
+                back = rims[x + 1, -1, dz]
+                total, along = total + back, -back if along is None else along - back
+            rims_out[side, pl.ds(x, 1), :] = total
+            rims_out[side, pl.ds(extent_x + x, 1), :] = along
+        sums.append(
+            send(rims_out.at[side], rims_in.at[side],
+                 halo_send.at[1, 2 + side], halo_recv.at[1, 2 + side], 0, dz)
+        )
+    for diagonal, (dx, dz) in enumerate(DIAGONALS):
+        tips_out[diagonal] = rims[last if dx > 0 else 0, dx, dz]
+        sums.append(
+            send(tips_out.at[diagonal], tips_in.at[diagonal],
+                 halo_send.at[1, 4 + diagonal], halo_recv.at[1, 4 + diagonal], dx, dz)
+        )
+    for x in outer_rows:
+        bounced(x)
     for x in range(extent_x):
-        f, fluid = streamed(1, x)
-        density = f[0]
-        forward = None
-        for i in range(1, 19, 2):
-            density = density + (f[i] + f[i + 1])
-            c = VELOCITIES[i][0]
-            if c:
-                term = (f[i] - f[i + 1])
-                forward = term if forward is None else forward + term
-        speed = walls[0, 1 + x, inner, :] * forward / density
+        total, along = density[x], forward[x]
+        if x > 0:
+            total, along = total + ahead[x - 1], along + ahead[x - 1]
+        if x < last:
+            total, along = total + behind[x + 1], along - behind[x + 1]
+        density[x] = total
+        forward[x] = along
+    for copy in sums:
+        copy.wait_recv()
+    for side, dz in enumerate((1, -1)):
+        row = 0 if dz > 0 else extent_z - 1
+        for x in range(extent_x):
+            total = rims_in[side, pl.ds(x, 1), :]
+            along = rims_in[side, pl.ds(extent_x + x, 1), :]
+            for diagonal, (cx, cz) in enumerate(DIAGONALS):
+                if cz == dz and x == (0 if cx > 0 else last):
+                    total = total + tips_in[diagonal]
+                    along = along + tips_in[diagonal] if cx > 0 else along - tips_in[diagonal]
+            density[x, pl.ds(row, 1), :] = density[x, pl.ds(row, 1), :] + total
+            forward[x, pl.ds(row, 1), :] = forward[x, pl.ds(row, 1), :] + along
+    for x in range(extent_x):
+        total, along = density[x], forward[x]
+        if x == 0:
+            total, along = total + sums_in[0], along + sums_in[0]
+        if x == last:
+            total, along = total + sums_in[1], along - sums_in[1]
+        speed = jnp.where(walls[0, 1 + x, inner, :] > 0, along / total, 0.0)
         if spectral:
             ux[pl.ds(x * extent_z, extent_z), :] = speed
         else:
@@ -363,6 +428,7 @@
             x_copies.append(copy)
         got_x[mx] = sent_x[mx]
         table_copy.wait()
+        first = weights[pl.ds(16, 128), :].astype(jnp.bfloat16)
         for copy in x_copies:
             copy.wait_recv()
         re, im = eight_point([got_x[s] for s in range(8)])
@@ -377,7 +443,6 @@
             left[pl.ds(k, 8, stride=8), :] = jnp.where(low_lanes, real, pltpu.roll(imag, 64, 1))
             left[pl.ds(64 + k, 8, stride=8), :] = jnp.where(low_lanes, pltpu.roll(real, 64, 1), imag)
         high, low = halves(left[...])
-        first = weights[pl.ds(16, 128), :].astype(jnp.bfloat16)
         contract = (((1,), (1,)), ((), ()))
         along = lax.dot_general(
             jnp.concatenate([first, first], axis=1),
@@ -414,7 +479,7 @@
         out_ref[1] = result[:, 64:].reshape(16, 8, 64)
         for copy in x_copies + z_copies:
             copy.wait_send()
-    for copy in finish + started:
+    for copy in x_sides + z_sides + corners + sums:
         copy.wait_send()
 
 
@@ -435,13 +500,22 @@
     scratch = [
         pltpu.VMEM((extent_x, 19, extent_z, height), f32),
         pltpu.VMEM((extent_x, extent_z, height), jnp.int32),
-        pltpu.VMEM((2, 19) + padded, f32),
+        pltpu.VMEM((19,) + padded, f32),
         pltpu.VMEM((19, extent_x, extent_z, height), f32),
         pltpu.VMEM((3,) + padded, f32),
-        pltpu.VMEM((2, 2, edge_rows, height), f32),
-        pltpu.VMEM((2, 2, edge_rows, height), f32),
-        pltpu.VMEM((2, 4, 2, height), f32),
-        pltpu.VMEM((2, 4, 2, height), f32),
+        pltpu.VMEM((2, edge_rows, height), f32),
+        pltpu.VMEM((2, edge_rows, height), f32),
+        pltpu.VMEM((4, 2, height), f32),
+        pltpu.VMEM((4, 2, height), f32),
+        pltpu.VMEM((2, extent_z, height), f32),
+        pltpu.VMEM((2, 2 * extent_x, height), f32),
+        pltpu.VMEM((2, 2 * extent_x, height), f32),
+        pltpu.VMEM((4, 1, height), f32),
+        pltpu.VMEM((4, 1, height), f32),
+        pltpu.VMEM((extent_x, extent_z, height), f32),
+        pltpu.VMEM((extent_x, extent_z, height), f32),
+        pltpu.VMEM((extent_x, extent_z, height), f32),
+        pltpu.VMEM((extent_x, extent_z, height), f32),
         dma((extent_x + 1,)),
         dma((2, 8)),
         dma((2, 8)),
@@ -466,11 +540,11 @@
         out_shape = jax.ShapeDtypeStruct((2, 16, 8, 64), f32)
     else:
         out_shape = jax.ShapeDtypeStruct((extent_x, extent_z, height), f32)
-    anywhere = pl.BlockSpec(memory_space=pl.ANY)
+    in_hbm = pl.BlockSpec(memory_space=pltpu.HBM)
     result = pl.pallas_call(
         functools.partial(kernel, spectral),
         out_shape=out_shape,
-        in_specs=[anywhere] * 3,
+        in_specs=[in_hbm] * 3,
         out_specs=pl.BlockSpec(memory_space=pltpu.VMEM),
         scratch_shapes=scratch,
         compiler_params=pltpu.CompilerParams(

time: 26.9 us -> 26 us (0.967)
  Pallas kernels: 23.3 us -> 22.4 us
    pallas_call x1, Pallas kernels: 23.3 us -> 22.4 us  [shards(): pl.pallas_call(functools.partial(kernel, spectral), out_shape=out_shape,...]
where the time goes in v2:
time: 26 us; the launch traced here: 25.8 us
  Pallas kernels  22.4 us (86%)
  local copies, waits for them, and re-layouts  3.4 us (13%)
    pallas_call x1, Pallas kernels, shards(): pl.pallas_call(functools.partial(kernel, spectral), out_shape=out_shape,...  22.4 us
    unnamed x7, local copies, waits for them, and re-layouts  3.4 us

profile of v2, /device:TPU:0, one launch (start us, length us, event | category | flops | bytes accessed | tf_op | source)
XLA Modules:
  0.0 25.8 jit_solution(9713144538953455673)
XLA Ops:
  0.0 0.0 copy-start
  0.0 1.1 %copy-done = f32[19,4,16,128]{3,2,1,0:T(8,128)S(1)} copy-done((f32[19,4,16,128]{3,2,1,0:T(8,128)S(1)}, f32[19,4,16,128]{3,2,1,0:T(8,128)}, u32[]{:S(2)}) %copy-start) | copy-done | bytes 622616
  1.1 0.0 copy-start.1
  1.1 0.9 %copy-done.1 = f32[272,128]{1,0:T(8,128)S(1)} copy-done((f32[272,128]{1,0:T(8,128)S(1)}, f32[272,128]{1,0:T(8,128)}, u32[]{:S(2)}) %copy-start.1) | copy-done | bytes 139288
  2.0 0.0 copy-start.2
  2.0 0.8 %copy-done.2 = s32[4,16,128]{2,1,0:T(8,128)S(1)} copy-done((s32[4,16,128]{2,1,0:T(8,128)S(1)}, s32[4,16,128]{2,1,0:T(8,128)}, u32[]{:S(2)}) %copy-start.2) | copy-done | bytes 32792
  2.7 22.4 %shard_map.37 = f32[2,16,8,64]{3,2,1,0:T(8,128)S(1)} custom-call(f32[19,4,16,128]{3,2,1,0:T(8,128)S(1)} %copy-done, s32[4,16,128]{2,1,0:T(8,128)S(1)} %copy-done.2, f32[272,128]{1,0:T(8,128)S(1)} %copy-done.1), custom_call_target="tpu_custom_call" | custom-call | tf_op jit(solution)/shard_map/pallas_call | solution.py:544
  25.1 0.7 %copy.5 = f32[2,16,8,64]{3,2,1,0:T(8,128)} copy(f32[2,16,8,64]{3,2,1,0:T(8,128)S(1)} %shard_map.37) | data formatting | bytes 131072
Async XLA Ops:
  0.0 1.1 %copy-start = (f32[19,4,16,128]{3,2,1,0:T(8,128)S(1)}, f32[19,4,16,128]{3,2,1,0:T(8,128)}, u32[]{:S(2)}) copy-start(f32[19,4,16,128]{3,2,1,0:T(8,128)} %populations.1) | copy-start | bytes 1867780
  1.1 0.9 %copy-start.1 = (f32[272,128]{1,0:T(8,128)S(1)}, f32[272,128]{1,0:T(8,128)}, u32[]{:S(2)}) copy-start(f32[272,128]{1,0:T(8,128)} %constant.2.clone.table) | copy-start | bytes 417796
  2.0 0.8 %copy-start.2 = (s32[4,16,128]{2,1,0:T(8,128)S(1)}, s32[4,16,128]{2,1,0:T(8,128)}, u32[]{:S(2)}) copy-start(s32[4,16,128]{2,1,0:T(8,128)} %fluid_mask.1) | copy-start | bytes 98308

commit v3 on v2

--- a/solution.py
+++ b/solution.py
@@ -548,7 +548,7 @@
         out_specs=pl.BlockSpec(memory_space=pltpu.VMEM),
         scratch_shapes=scratch,
         compiler_params=pltpu.CompilerParams(
-            collective_id=0, has_side_effects=True, vmem_limit_bytes=32 * 1024 * 1024
+            collective_id=0, has_side_effects=True
         ),
     )(populations, fluid_mask, table)
     if spectral:

time: 26 us -> 24.6 us (0.946)
  local copies, waits for them, and re-layouts: 3.4 us -> 1.57 us
  Pallas kernels: 22.4 us -> 22.9 us
    unnamed x7 -> x1, local copies, waits for them, and re-layouts: 3.4 us -> 1.57 us
    pallas_call x1, Pallas kernels: 22.4 us -> 22.9 us  [shards(): pl.pallas_call(functools.partial(kernel, spectral), out_shape=out_shape,...]
where the time goes in v3:
time: 24.6 us; the launch traced here: 24.5 us
  Pallas kernels  22.9 us (93%)
  local copies, waits for them, and re-layouts  1.57 us (6%)
    pallas_call x1, Pallas kernels, shards(): pl.pallas_call(functools.partial(kernel, spectral), out_shape=out_shape,...  22.9 us
    unnamed x1, local copies, waits for them, and re-layouts  1.57 us

profile of v3, /device:TPU:0, one launch (start us, length us, event | category | flops | bytes accessed | tf_op | source)
XLA Modules:
  0.0 24.5 jit_solution(11760152947208088705)
XLA Ops:
  0.0 22.9 %shard_map.37 = f32[2,16,8,64]{3,2,1,0:T(8,128)} custom-call(f32[19,4,16,128]{3,2,1,0:T(8,128)} %populations.1, s32[4,16,128]{2,1,0:T(8,128)} %fluid_mask.1, f32[272,128]{1,0:T(8,128)} %constant.2.clone.table), custom_call_target="tpu_custom_call" | custom-call | tf_op jit(solution)/shard_map/pallas_call | solution.py:544
  22.9 1.6 %copy.5 = f32[2,16,8,64]{3,2,1,0:T(8,128)} copy(f32[2,16,8,64]{3,2,1,0:T(8,128)} %shard_map.37) | data formatting | bytes 131072

commit v4 on v2

--- a/solution.py
+++ b/solution.py
@@ -550,7 +550,7 @@
         compiler_params=pltpu.CompilerParams(
             collective_id=0, has_side_effects=True, vmem_limit_bytes=32 * 1024 * 1024
         ),
-    )(populations, fluid_mask, table)
+    )(*(pltpu.with_memory_space_constraint(array, pltpu.HBM) for array in (populations, fluid_mask, table)))
     if spectral:
         return result
     return spectrum(result, norm_scale)

time: 26 us -> 23.1 us (0.89)
  local copies, waits for them, and re-layouts: 3.4 us -> 0.66 us
    unnamed x7 -> x1, local copies, waits for them, and re-layouts: 3.4 us -> 0.66 us
where the time goes in v4:
time: 23.1 us; the launch traced here: 22.9 us
  Pallas kernels  22.3 us (97%)
  local copies, waits for them, and re-layouts  0.66 us (3%)
    pallas_call x1, Pallas kernels, shards(): pl.pallas_call(functools.partial(kernel, spectral), out_shape=out_shape,...  22.3 us
    unnamed x1, local copies, waits for them, and re-layouts  0.66 us

profile of v4, /device:TPU:0, one launch (start us, length us, event | category | flops | bytes accessed | tf_op | source)
XLA Modules:
  0.0 22.9 jit_solution(16828629092051694335)
XLA Ops:
  0.0 22.3 %shard_map.37 = f32[2,16,8,64]{3,2,1,0:T(8,128)S(1)} custom-call(f32[19,4,16,128]{3,2,1,0:T(8,128)} %populations.1, s32[4,16,128]{2,1,0:T(8,128)} %fluid_mask.1, f32[272,128]{1,0:T(8,128)} %constant.2.clone.table), custom_call_target="tpu_custom_call" | custom-call | tf_op jit(solution)/shard_map/pallas_call | solution.py:544
  22.3 0.7 %copy.5 = f32[2,16,8,64]{3,2,1,0:T(8,128)} copy(f32[2,16,8,64]{3,2,1,0:T(8,128)S(1)} %shard_map.37) | data formatting | bytes 131072

commit v5 on v4

--- a/solution.py
+++ b/solution.py
@@ -43,6 +43,7 @@
 SIDES = ((1, 0), (-1, 0), (0, 1), (0, -1))
 DIAGONALS = ((1, 1), (1, -1), (-1, 1), (-1, -1))
 DIAGONAL_SLOT = (4, 0, 8, 12)
+RIM = {(cx, cz): 2 * (cx + 1) + (cz + 1) // 2 for cx in (-1, 0, 1) for cz in (-1, 1)}
 TOP = 8
 MESH = pl.DeviceIdType.MESH
 
@@ -146,11 +147,11 @@
 
 def kernel(spectral, populations, fluid_mask, table, *rest):
     (out_ref, held, mask_i, rolled, plain, walls, edges_out, edges_in, corners_out, corners_in,
-     sums_in, rims_out, rims_in, tips_out, tips_in, density, forward, ahead, behind,
-     in_sem, halo_send, halo_recv, mask_send, mask_recv) = rest[:24]
+     sums_in, rims_out, rims_in, tips_out, tips_in, density, forward, ahead, behind, rims,
+     in_sem, halo_send, halo_recv, mask_send, mask_recv) = rest[:25]
     if spectral:
         (ux, sent_x, got_x, left, sent_z, got_z, weights,
-         table_sem, x_send, x_recv, z_send, z_recv) = rest[24:]
+         table_sem, x_send, x_recv, z_send, z_recv) = rest[25:]
     extent_x, extent_z, height = fluid_mask.shape
     last = extent_x - 1
     count_x, count_z = lax.axis_size("gx"), lax.axis_size("gz")
@@ -163,15 +164,14 @@
         return lax.rem(mz + step + count_z, count_z)
 
     inner = pl.ds(TOP, extent_z)
-    outer_rows = (0, last)
-    inner_rows = tuple(range(1, last))
+
+    def fetch(x):
+        return pltpu.make_async_copy(populations.at[:, x], held.at[x], in_sem.at[x])
 
     mask_copy = pltpu.make_async_copy(fluid_mask, mask_i, in_sem.at[extent_x])
     mask_copy.start()
-    fetches = {}
-    for x in outer_rows + inner_rows:
-        fetches[x] = pltpu.make_async_copy(populations.at[:, x], held.at[x], in_sem.at[x])
-        fetches[x].start()
+    for k in range(extent_x):
+        fetch((extent_x - k) % extent_x).start()
 
     barrier = pltpu.get_barrier_semaphore()
     partners = [(shifted_x(dx), shifted_z(dz)) for dx, dz in SIDES + DIAGONALS]
@@ -191,33 +191,8 @@
         row = extent_z - 1 if cz > 0 else 0
         return value[row : row + 1, :]
 
-    def first_collision(x):
-        fetches[x].wait()
-        solid = mask_i[x].astype(jnp.float32)
-        walls[0, 1 + x, inner, :] = solid
-        for side, cz in enumerate((1, -1)):
-            edges_out[side, pl.ds(5 * extent_x + x, 1), :] = edge_of(solid, cz)
-        for diagonal, (cx, cz) in enumerate(DIAGONALS):
-            if x == (last if cx > 0 else 0):
-                corners_out[diagonal, pl.ds(1, 1), :] = edge_of(solid, cz)
-        g = collide([held[x, number] for number in range(19)], solid > 0)
-        for number in range(19):
-            cx, cy, cz = VELOCITIES[number]
-            value = g[number]
-            if cy:
-                plain[number, x] = value
-                value = pltpu.roll(value, cy % height, 1)
-            slot = SLOT[number]
-            rolled[slot, 1 + x, inner, :] = value
-            if cz:
-                order = (slot - Z_FIRST[cz]) % 16
-                edge = edge_of(value, cz)
-                edges_out[0 if cz > 0 else 1, pl.ds(order * extent_x + x, 1), :] = edge
-                if cx and x == (last if cx > 0 else 0):
-                    corners_out[DIAGONALS.index((cx, cz)), pl.ds(0, 1), :] = edge
-
-    def send(source, target, send_sem, recv_sem, dx, dz):
-        copy = pltpu.make_async_remote_copy(
+    def remote(source, target, send_sem, recv_sem, dx, dz):
+        return pltpu.make_async_remote_copy(
             src_ref=source,
             dst_ref=target,
             send_sem=send_sem,
@@ -225,33 +200,68 @@
             device_id=(shifted_x(dx), shifted_z(dz)),
             device_id_type=MESH,
         )
+
+    def send(*arguments):
+        copy = remote(*arguments)
         copy.start()
         return copy
 
-    mask_copy.wait()
-    for x in outer_rows:
-        first_collision(x)
-    pl.semaphore_wait(barrier, len(partners))
-    x_sides, z_sides, corners = [], [], []
+    x_sides = []
     for side, dx in enumerate((1, -1)):
         here, there = (extent_x, 0) if dx > 0 else (1, extent_x + 1)
         group = pl.ds(X_FIRST[dx], 5)
         x_sides.append(
-            send(rolled.at[group, here, inner], rolled.at[group, there, inner],
-                 halo_send.at[0, side], halo_recv.at[0, side], dx, 0)
+            remote(rolled.at[group, here, inner], rolled.at[group, there, inner],
+                   halo_send.at[0, side], halo_recv.at[0, side], dx, 0)
         )
         x_sides.append(
-            send(walls.at[0, here, inner], walls.at[0, there, inner],
-                 mask_send.at[side], mask_recv.at[side], dx, 0)
-        )
-    for x in inner_rows:
-        first_collision(x)
-    for side, dz in enumerate((1, -1)):
+            remote(walls.at[0, here, inner], walls.at[0, there, inner],
+                   mask_send.at[side], mask_recv.at[side], dx, 0)
+        )
+
+    mask_copy.wait()
+    for x in range(extent_x):
+        walls[0, 1 + x, inner, :] = mask_i[x].astype(jnp.float32)
+
+    def first_collision(k, carry):
+        x = lax.rem(extent_x - k, extent_x)
+        fetch(x).wait()
+        g = collide([held[x, number] for number in range(19)], walls[0, 1 + x, inner, :] > 0)
+        for number in range(19):
+            cy = VELOCITIES[number][1]
+            value = g[number]
+            if cy:
+                plain[number, x] = value
+                value = pltpu.roll(value, cy % height, 1)
+            rolled[SLOT[number], 1 + x, inner, :] = value
+
+        @pl.when(k == 1)
+        def _():
+            pl.semaphore_wait(barrier, len(partners))
+            for copy in x_sides:
+                copy.start()
+
+        return carry
+
+    lax.fori_loop(0, extent_x, first_collision, 0)
+    z_sides, corners = [], []
+    for side, cz in enumerate((1, -1)):
+        row = pl.ds(TOP + extent_z - 1 if cz > 0 else TOP, 1)
+        for x in range(extent_x):
+            for order in range(5):
+                edges_out[side, pl.ds(order * extent_x + x, 1), :] = rolled[
+                    (Z_FIRST[cz] + order) % 16, 1 + x, row, :
+                ]
+            edges_out[side, pl.ds(5 * extent_x + x, 1), :] = walls[0, 1 + x, row, :]
         z_sides.append(
             send(edges_out.at[side], edges_in.at[side],
-                 halo_send.at[0, 2 + side], halo_recv.at[0, 2 + side], 0, dz)
+                 halo_send.at[0, 2 + side], halo_recv.at[0, 2 + side], 0, cz)
         )
     for diagonal, (dx, dz) in enumerate(DIAGONALS):
+        row = pl.ds(TOP + extent_z - 1 if dz > 0 else TOP, 1)
+        plane = extent_x if dx > 0 else 1
+        corners_out[diagonal, pl.ds(0, 1), :] = rolled[DIAGONAL_SLOT[diagonal], plane, row, :]
+        corners_out[diagonal, pl.ds(1, 1), :] = walls[0, plane, row, :]
         corners.append(
             send(corners_out.at[diagonal], corners_in.at[diagonal],
                  halo_send.at[0, 4 + diagonal], halo_recv.at[0, 4 + diagonal], dx, dz)
@@ -268,7 +278,22 @@
         cx, cy, cz = VELOCITIES[number]
         return walls[(0, 1, 2)[cy], 1 + x - cx, pl.ds(TOP - cz, extent_z), :] > 0
 
-    def streamed(x, fluid):
+    def second_collision(k, carry):
+        x = lax.rem(k + 1, extent_x)
+
+        @pl.when(k == extent_x - 2)
+        def _():
+            for copy in x_sides + corners:
+                copy.wait_recv()
+            for diagonal, (cx, cz) in enumerate(DIAGONALS):
+                plane = 0 if cx > 0 else extent_x + 1
+                row = pl.ds(TOP - 1 if cz > 0 else TOP + extent_z, 1)
+                rolled[DIAGONAL_SLOT[diagonal], plane, row, :] = corners_in[diagonal, pl.ds(0, 1), :]
+                walls[0, plane, row, :] = corners_in[diagonal, pl.ds(1, 1), :]
+            for plane in (0, extent_x + 1):
+                shift_walls(plane)
+
+        fluid = walls[0, 1 + x, inner, :] > 0
         owned = []
         for number in range(19):
             if VELOCITIES[number][1]:
@@ -281,16 +306,9 @@
             value = rolled[SLOT[number], 1 + x - cx, pl.ds(TOP - cz, extent_z), :]
             arrived = jnp.where(wall_from(number, x), value, owned[OPPOSITES[number]])
             f.append(jnp.where(fluid, arrived, owned[number]))
-        return f
-
-    rims = {}
-
-    def second_collision(x):
-        fluid = walls[0, 1 + x, inner, :] > 0
-        g = collide(streamed(x, fluid), fluid)
-        for number in range(19):
-            held[x, number] = g[number]
+        g = collide(f, fluid)
         leaving = {}
+        turned_back = {}
         for number in range(1, 19):
             cx, cy, cz = VELOCITIES[number]
             value = jnp.where(fluid, g[number], 0.0)
@@ -298,53 +316,39 @@
                 value = pltpu.roll(value, cy % height, 1)
                 value = jnp.where(lanes == (0 if cy > 0 else height - 1), 0.0, value)
             leaving[cx, cz] = leaving[cx, cz] + value if (cx, cz) in leaving else value
+            value = jnp.where(wall_from(number, x), 0.0, g[OPPOSITES[number]])
+            turned_back[cx] = turned_back[cx] + value if cx in turned_back else value
         for cx, keep in ((1, ahead), (-1, behind), (0, None)):
             total = leaving[cx, 0]
             for cz in (1, -1):
                 value = leaving[cx, cz]
-                rims[x, cx, cz] = edge_of(value, cz)
+                rims[RIM[cx, cz], x] = edge_of(value, cz)
                 moved = pltpu.roll(value, cz % extent_z, 0)
                 total = total + jnp.where(rows == (0 if cz > 0 else extent_z - 1), 0.0, moved)
             if keep is None:
-                density[x] = g[0] + total
+                density[x] = (g[0] + total) + (turned_back[0] + turned_back[1] + turned_back[-1])
             else:
                 keep[x] = total
-
-    def bounced(x):
-        sums = {}
-        for number in range(1, 19):
-            cx = VELOCITIES[number][0]
-            value = jnp.where(wall_from(number, x), 0.0, held[x, OPPOSITES[number]])
-            sums[cx] = sums[cx] + value if cx in sums else value
-        density[x] = density[x] + (sums[0] + sums[1] + sums[-1])
-        forward[x] = sums[1] - sums[-1]
+        forward[x] = turned_back[1] - turned_back[-1]
+        return carry
 
     for copy in z_sides:
         copy.wait_recv()
     for side, cz in enumerate((1, -1)):
-        row = TOP - 1 if cz > 0 else TOP + extent_z
+        row = pl.ds(TOP - 1 if cz > 0 else TOP + extent_z, 1)
         for x in range(extent_x):
             for order in range(5):
-                rolled[(Z_FIRST[cz] + order) % 16, 1 + x, pl.ds(row, 1), :] = edges_in[
+                rolled[(Z_FIRST[cz] + order) % 16, 1 + x, row, :] = edges_in[
                     side, pl.ds(order * extent_x + x, 1), :
                 ]
-            walls[0, 1 + x, pl.ds(row, 1), :] = edges_in[side, pl.ds(5 * extent_x + x, 1), :]
-    for x in range(extent_x):
-        shift_walls(1 + x)
-    for x in inner_rows:
-        second_collision(x)
-        bounced(x)
-    for copy in x_sides + corners:
-        copy.wait_recv()
-    for diagonal, (cx, cz) in enumerate(DIAGONALS):
-        plane = 0 if cx > 0 else extent_x + 1
-        row = TOP - 1 if cz > 0 else TOP + extent_z
-        rolled[DIAGONAL_SLOT[diagonal], plane, pl.ds(row, 1), :] = corners_in[diagonal, pl.ds(0, 1), :]
-        walls[0, plane, pl.ds(row, 1), :] = corners_in[diagonal, pl.ds(1, 1), :]
-    for plane in (0, extent_x + 1):
+            walls[0, 1 + x, row, :] = edges_in[side, pl.ds(5 * extent_x + x, 1), :]
+
+    def shift_inner(plane, carry):
         shift_walls(plane)
-    for x in outer_rows:
-        second_collision(x)
+        return carry
+
+    lax.fori_loop(1, 1 + extent_x, shift_inner, 0)
+    lax.fori_loop(0, extent_x, second_collision, 0)
 
     sums = []
     for side, (dx, x, keep) in enumerate(((1, last, ahead), (-1, 0, behind))):
@@ -354,11 +358,11 @@
         )
     for side, dz in enumerate((1, -1)):
         for x in range(extent_x):
-            total, along = rims[x, 0, dz], None
+            total, along = rims[RIM[0, dz], x], None
             if x > 0:
-                total, along = total + rims[x - 1, 1, dz], rims[x - 1, 1, dz]
+                total, along = total + rims[RIM[1, dz], x - 1], rims[RIM[1, dz], x - 1]
             if x < last:
-                back = rims[x + 1, -1, dz]
+                back = rims[RIM[-1, dz], x + 1]
                 total, along = total + back, -back if along is None else along - back
             rims_out[side, pl.ds(x, 1), :] = total
             rims_out[side, pl.ds(extent_x + x, 1), :] = along
@@ -367,13 +371,11 @@
                  halo_send.at[1, 2 + side], halo_recv.at[1, 2 + side], 0, dz)
         )
     for diagonal, (dx, dz) in enumerate(DIAGONALS):
-        tips_out[diagonal] = rims[last if dx > 0 else 0, dx, dz]
+        tips_out[diagonal] = rims[RIM[dx, dz], last if dx > 0 else 0]
         sums.append(
             send(tips_out.at[diagonal], tips_in.at[diagonal],
                  halo_send.at[1, 4 + diagonal], halo_recv.at[1, 4 + diagonal], dx, dz)
         )
-    for x in outer_rows:
-        bounced(x)
     for x in range(extent_x):
         total, along = density[x], forward[x]
         if x > 0:
@@ -516,6 +518,7 @@
         pltpu.VMEM((extent_x, extent_z, height), f32),
         pltpu.VMEM((extent_x, extent_z, height), f32),
         pltpu.VMEM((extent_x, extent_z, height), f32),
+        pltpu.VMEM((6, extent_x, 1, height), f32),
         dma((extent_x + 1,)),
         dma((2, 8)),
         dma((2, 8)),

time: 23.1 us -> 23.4 us (1.013)
    pallas_call x1, Pallas kernels: 22.3 us -> 22.5 us  [shards(): pl.pallas_call(functools.partial(kernel, spectral), out_shape=out_shape,...]
where the time goes in v5:
time: 23.4 us; the launch traced here: 23.2 us
  Pallas kernels  22.5 us (96%)
  local copies, waits for them, and re-layouts  0.66 us (3%)
    pallas_call x1, Pallas kernels, shards(): pl.pallas_call(functools.partial(kernel, spectral), out_shape=out_shape,...  22.5 us
    unnamed x1, local copies, waits for them, and re-layouts  0.66 us

profile of v5, /device:TPU:0, one launch (start us, length us, event | category | flops | bytes accessed | tf_op | source)
XLA Modules:
  0.0 23.2 jit_solution(6277969096598188406)
XLA Ops:
  0.0 22.5 %shard_map.37 = f32[2,16,8,64]{3,2,1,0:T(8,128)S(1)} custom-call(f32[19,4,16,128]{3,2,1,0:T(8,128)} %populations.1, s32[4,16,128]{2,1,0:T(8,128)} %fluid_mask.1, f32[272,128]{1,0:T(8,128)} %constant.2.clone.table), custom_call_target="tpu_custom_call" | custom-call | tf_op jit(solution)/shard_map/pallas_call | solution.py:547
  22.6 0.7 %copy.5 = f32[2,16,8,64]{3,2,1,0:T(8,128)} copy(f32[2,16,8,64]{3,2,1,0:T(8,128)S(1)} %shard_map.37) | data formatting | bytes 131072

commit v6 on v5

--- a/solution.py
+++ b/solution.py
@@ -147,11 +147,11 @@
 
 def kernel(spectral, populations, fluid_mask, table, *rest):
     (out_ref, held, mask_i, rolled, plain, walls, edges_out, edges_in, corners_out, corners_in,
-     sums_in, rims_out, rims_in, tips_out, tips_in, density, forward, ahead, behind, rims,
-     in_sem, halo_send, halo_recv, mask_send, mask_recv) = rest[:25]
+     sums_in, rims_out, rims_in, density, forward, ahead, behind, rims,
+     in_sem, halo_send, halo_recv, mask_send, mask_recv) = rest[:23]
     if spectral:
-        (ux, sent_x, got_x, left, sent_z, got_z, weights,
-         table_sem, x_send, x_recv, z_send, z_recv) = rest[25:]
+        (sent_x, got_x, left, sent_z, got_z, weights,
+         table_sem, x_send, x_recv, z_send, z_recv) = rest[23:]
     extent_x, extent_z, height = fluid_mask.shape
     last = extent_x - 1
     count_x, count_z = lax.axis_size("gx"), lax.axis_size("gz")
@@ -350,31 +350,23 @@
     lax.fori_loop(1, 1 + extent_x, shift_inner, 0)
     lax.fori_loop(0, extent_x, second_collision, 0)
 
-    sums = []
-    for side, (dx, x, keep) in enumerate(((1, last, ahead), (-1, 0, behind))):
-        sums.append(
-            send(keep.at[x], sums_in.at[side],
-                 halo_send.at[1, side], halo_recv.at[1, side], dx, 0)
-        )
+    rim_copies = []
     for side, dz in enumerate((1, -1)):
         for x in range(extent_x):
             total, along = rims[RIM[0, dz], x], None
             if x > 0:
-                total, along = total + rims[RIM[1, dz], x - 1], rims[RIM[1, dz], x - 1]
+                forth = rims[RIM[1, dz], x - 1]
+                total, along = total + forth, forth
             if x < last:
                 back = rims[RIM[-1, dz], x + 1]
                 total, along = total + back, -back if along is None else along - back
             rims_out[side, pl.ds(x, 1), :] = total
             rims_out[side, pl.ds(extent_x + x, 1), :] = along
-        sums.append(
+        rims_out[side, pl.ds(2 * extent_x, 1), :] = rims[RIM[1, dz], last]
+        rims_out[side, pl.ds(2 * extent_x + 1, 1), :] = rims[RIM[-1, dz], 0]
+        rim_copies.append(
             send(rims_out.at[side], rims_in.at[side],
-                 halo_send.at[1, 2 + side], halo_recv.at[1, 2 + side], 0, dz)
-        )
-    for diagonal, (dx, dz) in enumerate(DIAGONALS):
-        tips_out[diagonal] = rims[RIM[dx, dz], last if dx > 0 else 0]
-        sums.append(
-            send(tips_out.at[diagonal], tips_in.at[diagonal],
-                 halo_send.at[1, 4 + diagonal], halo_recv.at[1, 4 + diagonal], dx, dz)
+                 halo_send.at[1, side], halo_recv.at[1, side], 0, dz)
         )
     for x in range(extent_x):
         total, along = density[x], forward[x]
@@ -384,37 +376,50 @@
             total, along = total + behind[x + 1], along - behind[x + 1]
         density[x] = total
         forward[x] = along
-    for copy in sums:
+    for copy in rim_copies:
         copy.wait_recv()
     for side, dz in enumerate((1, -1)):
-        row = 0 if dz > 0 else extent_z - 1
+        row = pl.ds(0 if dz > 0 else extent_z - 1, 1)
         for x in range(extent_x):
-            total = rims_in[side, pl.ds(x, 1), :]
-            along = rims_in[side, pl.ds(extent_x + x, 1), :]
-            for diagonal, (cx, cz) in enumerate(DIAGONALS):
-                if cz == dz and x == (0 if cx > 0 else last):
-                    total = total + tips_in[diagonal]
-                    along = along + tips_in[diagonal] if cx > 0 else along - tips_in[diagonal]
-            density[x, pl.ds(row, 1), :] = density[x, pl.ds(row, 1), :] + total
-            forward[x, pl.ds(row, 1), :] = forward[x, pl.ds(row, 1), :] + along
-    for x in range(extent_x):
-        total, along = density[x], forward[x]
-        if x == 0:
-            total, along = total + sums_in[0], along + sums_in[0]
-        if x == last:
-            total, along = total + sums_in[1], along - sums_in[1]
-        speed = jnp.where(walls[0, 1 + x, inner, :] > 0, along / total, 0.0)
-        if spectral:
-            ux[pl.ds(x * extent_z, extent_z), :] = speed
-        else:
-            out_ref[x] = speed
+            density[x, row, :] = density[x, row, :] + rims_in[side, pl.ds(x, 1), :]
+            forward[x, row, :] = forward[x, row, :] + rims_in[side, pl.ds(extent_x + x, 1), :]
+        ahead[last, row, :] = ahead[last, row, :] + rims_in[side, pl.ds(2 * extent_x, 1), :]
+        behind[0, row, :] = behind[0, row, :] + rims_in[side, pl.ds(2 * extent_x + 1, 1), :]
+
+    def is_fluid(plane):
+        return walls[0, plane, inner, :] > 0
+
+    if not spectral:
+        sums = []
+        for side, (dx, x, keep) in enumerate(((1, last, ahead), (-1, 0, behind))):
+            sums.append(
+                send(keep.at[x], sums_in.at[side],
+                     halo_send.at[1, 2 + side], halo_recv.at[1, 2 + side], dx, 0)
+            )
+        for copy in sums:
+            copy.wait_recv()
+        for x in range(extent_x):
+            total, along = density[x], forward[x]
+            if x == 0:
+                total, along = total + sums_in[0], along + sums_in[0]
+            if x == last:
+                total, along = total + sums_in[1], along - sums_in[1]
+            out_ref[x] = jnp.where(is_fluid(1 + x), along / total, 0.0)
+        for copy in rim_copies + sums:
+            copy.wait_send()
 
     if spectral:
-        whole = ux[...]
-        both = jnp.concatenate([whole, pltpu.roll(whole, height - 8, 1)], axis=0)
-        turned = both.T
-        for a in range(count_x):
-            sent_x[a] = turned[16 * a : 16 * a + 8, :]
+        parts = []
+        for x in range(extent_x):
+            if x in (0, last):
+                parts.append(jnp.where(is_fluid(1 + x), density[x], 1.0))
+            else:
+                parts.append(jnp.where(is_fluid(1 + x), forward[x] / density[x], 0.0))
+        parts.append(jnp.where(is_fluid(1), forward[0], 0.0))
+        parts.append(jnp.where(is_fluid(extent_x + 1), ahead[last], 0.0))
+        parts.append(jnp.where(is_fluid(0), behind[0], 0.0))
+        parts.append(jnp.where(is_fluid(extent_x), forward[last], 0.0))
+        sent_x[...] = jnp.concatenate(parts, axis=0).T.reshape(8, 16, 128)
         x_copies = []
         for p in range(1, count_x):
             there = shifted_x(p)
@@ -433,8 +438,19 @@
         first = weights[pl.ds(16, 128), :].astype(jnp.bfloat16)
         for copy in x_copies:
             copy.wait_recv()
-        re, im = eight_point([got_x[s] for s in range(8)])
-        low_lanes = lax.broadcasted_iota(jnp.int32, (8, 128), 1) < 64
+        lane = lax.broadcasted_iota(jnp.int32, (16, 128), 1)
+        head, tail = lane < 16, lane >= 48
+        got = [got_x[s] for s in range(8)]
+        speeds = []
+        for s in range(8):
+            forth = pltpu.roll(got[(s - 1) % 8], 128 - 80, 1)
+            back = pltpu.roll(got[(s + 1) % 8], 128 - 48, 1)
+            mine = pltpu.roll(got[s], 64, 1)
+            total = got[s] + jnp.where(head, forth, back)
+            along = mine + jnp.where(head, forth, -back)
+            speeds.append(jnp.where(head | tail, along / total, got[s]))
+        re, im = eight_point(speeds)
+        low_lanes = lane < 64
         for k in range(8):
             c = weights[pl.ds(k, 1), :]
             s = weights[pl.ds(8 + k, 1), :]
@@ -442,8 +458,7 @@
                 real, imag = re[k] * c, -re[k] * s
             else:
                 real, imag = re[k] * c + im[k] * s, im[k] * c - re[k] * s
-            left[pl.ds(k, 8, stride=8), :] = jnp.where(low_lanes, real, pltpu.roll(imag, 64, 1))
-            left[pl.ds(64 + k, 8, stride=8), :] = jnp.where(low_lanes, pltpu.roll(real, 64, 1), imag)
+            left[pl.ds(k, 16, stride=8), :] = jnp.where(low_lanes, real, pltpu.roll(imag, 64, 1))
         high, low = halves(left[...])
         contract = (((1,), (1,)), ((), ()))
         along = lax.dot_general(
@@ -479,9 +494,9 @@
         ) + jnp.dot(high, second_low, preferred_element_type=jnp.float32)
         out_ref[0] = result[:, :64].reshape(16, 8, 64)
         out_ref[1] = result[:, 64:].reshape(16, 8, 64)
-        for copy in x_copies + z_copies:
+        for copy in rim_copies + x_copies + z_copies:
             copy.wait_send()
-    for copy in x_sides + z_sides + corners + sums:
+    for copy in x_sides + z_sides + corners:
         copy.wait_send()
 
 
@@ -510,10 +525,8 @@
         pltpu.VMEM((4, 2, height), f32),
         pltpu.VMEM((4, 2, height), f32),
         pltpu.VMEM((2, extent_z, height), f32),
-        pltpu.VMEM((2, 2 * extent_x, height), f32),
-        pltpu.VMEM((2, 2 * extent_x, height), f32),
-        pltpu.VMEM((4, 1, height), f32),
-        pltpu.VMEM((4, 1, height), f32),
+        pltpu.VMEM((2, 2 * extent_x + 2, height), f32),
+        pltpu.VMEM((2, 2 * extent_x + 2, height), f32),
         pltpu.VMEM((extent_x, extent_z, height), f32),
         pltpu.VMEM((extent_x, extent_z, height), f32),
         pltpu.VMEM((extent_x, extent_z, height), f32),
@@ -527,9 +540,8 @@
     ]
     if spectral:
         scratch += [
-            pltpu.VMEM((64, 128), f32),
-            pltpu.VMEM((8, 8, 128), f32),
-            pltpu.VMEM((8, 8, 128), f32),
+            pltpu.VMEM((8, 16, 128), f32),
+            pltpu.VMEM((8, 16, 128), f32),
             pltpu.VMEM((128, 128), f32),
             pltpu.VMEM((4, 32, 128), f32),
             pltpu.VMEM((4, 32, 128), f32),

time: 23.4 us -> 22.8 us (0.974)
  Pallas kernels: 22.5 us -> 22 us
    pallas_call x1, Pallas kernels: 22.5 us -> 22 us  [shards(): pl.pallas_call(functools.partial(kernel, spectral), out_shape=out_shape,...]
where the time goes in v6:
time: 22.8 us; the launch traced here: 22.7 us
  Pallas kernels  22 us (96%)
  local copies, waits for them, and re-layouts  0.66 us (3%)
    pallas_call x1, Pallas kernels, shards(): pl.pallas_call(functools.partial(kernel, spectral), out_shape=out_shape,...  22 us
    unnamed x1, local copies, waits for them, and re-layouts  0.66 us

profile of v6, /device:TPU:0, one launch (start us, length us, event | category | flops | bytes accessed | tf_op | source)
XLA Modules:
  0.0 22.7 jit_solution(11660496896817635671)
XLA Ops:
  0.0 22.0 %shard_map.37 = f32[2,16,8,64]{3,2,1,0:T(8,128)S(1)} custom-call(f32[19,4,16,128]{3,2,1,0:T(8,128)} %populations.1, s32[4,16,128]{2,1,0:T(8,128)} %fluid_mask.1, f32[272,128]{1,0:T(8,128)} %constant.2.clone.table), custom_call_target="tpu_custom_call" | custom-call | tf_op jit(solution)/shard_map/pallas_call | solution.py:559
  22.0 0.7 %copy.5 = f32[2,16,8,64]{3,2,1,0:T(8,128)} copy(f32[2,16,8,64]{3,2,1,0:T(8,128)S(1)} %shard_map.37) | data formatting | bytes 131072

commit v7 on v6

--- a/solution.py
+++ b/solution.py
@@ -43,7 +43,6 @@
 SIDES = ((1, 0), (-1, 0), (0, 1), (0, -1))
 DIAGONALS = ((1, 1), (1, -1), (-1, 1), (-1, -1))
 DIAGONAL_SLOT = (4, 0, 8, 12)
-RIM = {(cx, cz): 2 * (cx + 1) + (cz + 1) // 2 for cx in (-1, 0, 1) for cz in (-1, 1)}
 TOP = 8
 MESH = pl.DeviceIdType.MESH
 
@@ -147,11 +146,11 @@
 
 def kernel(spectral, populations, fluid_mask, table, *rest):
     (out_ref, held, mask_i, rolled, plain, walls, edges_out, edges_in, corners_out, corners_in,
-     sums_in, rims_out, rims_in, density, forward, ahead, behind, rims,
-     in_sem, halo_send, halo_recv, mask_send, mask_recv) = rest[:23]
+     sums_in, density, forward, ahead, behind,
+     in_sem, halo_send, halo_recv, mask_send, mask_recv) = rest[:20]
     if spectral:
         (sent_x, got_x, left, sent_z, got_z, weights,
-         table_sem, x_send, x_recv, z_send, z_recv) = rest[23:]
+         table_sem, x_send, x_recv, z_send, z_recv) = rest[20:]
     extent_x, extent_z, height = fluid_mask.shape
     last = extent_x - 1
     count_x, count_z = lax.axis_size("gx"), lax.axis_size("gz")
@@ -184,12 +183,18 @@
         table_copy = pltpu.make_async_copy(table, weights, table_sem.at[0])
         table_copy.start()
 
-    lanes = lax.broadcasted_iota(jnp.int32, (extent_z, height), 1)
-    rows = lax.broadcasted_iota(jnp.int32, (extent_z, height), 0)
-
-    def edge_of(value, cz):
-        row = extent_z - 1 if cz > 0 else 0
-        return value[row : row + 1, :]
+    wide = extent_z + 2
+    lanes = lax.broadcasted_iota(jnp.int32, (wide, height), 1)
+
+    def edge_rows(cz):
+        if cz > 0:
+            return pl.ds(TOP + extent_z - 1, 1), pl.ds(TOP + extent_z - 2, 1)
+        return pl.ds(TOP, 1), pl.ds(TOP + 1, 1)
+
+    def halo_rows(cz):
+        if cz > 0:
+            return pl.ds(TOP - 1, 1), pl.ds(TOP - 2, 1)
+        return pl.ds(TOP + extent_z, 1), pl.ds(TOP + extent_z + 1, 1)
 
     def remote(source, target, send_sem, recv_sem, dx, dz):
         return pltpu.make_async_remote_copy(
@@ -206,7 +211,7 @@
         copy.start()
         return copy
 
-    x_sides = []
+    x_sides, x_masks = [], []
     for side, dx in enumerate((1, -1)):
         here, there = (extent_x, 0) if dx > 0 else (1, extent_x + 1)
         group = pl.ds(X_FIRST[dx], 5)
@@ -214,7 +219,7 @@
             remote(rolled.at[group, here, inner], rolled.at[group, there, inner],
                    halo_send.at[0, side], halo_recv.at[0, side], dx, 0)
         )
-        x_sides.append(
+        x_masks.append(
             remote(walls.at[0, here, inner], walls.at[0, there, inner],
                    mask_send.at[side], mask_recv.at[side], dx, 0)
         )
@@ -231,37 +236,52 @@
             cy = VELOCITIES[number][1]
             value = g[number]
             if cy:
-                plain[number, x] = value
+                plain[number, x, inner, :] = value
                 value = pltpu.roll(value, cy % height, 1)
             rolled[SLOT[number], 1 + x, inner, :] = value
 
         @pl.when(k == 1)
         def _():
             pl.semaphore_wait(barrier, len(partners))
-            for copy in x_sides:
+            for copy in x_sides + x_masks:
                 copy.start()
 
         return carry
 
     lax.fori_loop(0, extent_x, first_collision, 0)
     z_sides, corners = [], []
+
+    def pack(x, carry):
+        for side, cz in enumerate((1, -1)):
+            edge, beside = edge_rows(cz)
+            for number in range(19):
+                if VELOCITIES[number][1]:
+                    value = plain[number, x, edge, :]
+                else:
+                    value = rolled[SLOT[number], 1 + x, edge, :]
+                edges_out[side, x, pl.ds(number, 1), :] = value
+            for order in range(5):
+                edges_out[side, x, pl.ds(19 + order, 1), :] = rolled[
+                    (Z_FIRST[cz] + order) % 16, 1 + x, beside, :
+                ]
+            edges_out[side, x, pl.ds(24, 1), :] = walls[0, 1 + x, edge, :]
+            edges_out[side, x, pl.ds(25, 1), :] = walls[0, 1 + x, beside, :]
+        return carry
+
+    lax.fori_loop(0, extent_x, pack, 0)
     for side, cz in enumerate((1, -1)):
-        row = pl.ds(TOP + extent_z - 1 if cz > 0 else TOP, 1)
-        for x in range(extent_x):
-            for order in range(5):
-                edges_out[side, pl.ds(order * extent_x + x, 1), :] = rolled[
-                    (Z_FIRST[cz] + order) % 16, 1 + x, row, :
-                ]
-            edges_out[side, pl.ds(5 * extent_x + x, 1), :] = walls[0, 1 + x, row, :]
         z_sides.append(
             send(edges_out.at[side], edges_in.at[side],
                  halo_send.at[0, 2 + side], halo_recv.at[0, 2 + side], 0, cz)
         )
     for diagonal, (dx, dz) in enumerate(DIAGONALS):
-        row = pl.ds(TOP + extent_z - 1 if dz > 0 else TOP, 1)
+        edge, beside = edge_rows(dz)
         plane = extent_x if dx > 0 else 1
-        corners_out[diagonal, pl.ds(0, 1), :] = rolled[DIAGONAL_SLOT[diagonal], plane, row, :]
-        corners_out[diagonal, pl.ds(1, 1), :] = walls[0, plane, row, :]
+        for order in range(5):
+            corners_out[diagonal, pl.ds(order, 1), :] = rolled[X_FIRST[dx] + order, plane, edge, :]
+        corners_out[diagonal, pl.ds(5, 1), :] = rolled[DIAGONAL_SLOT[diagonal], plane, beside, :]
+        corners_out[diagonal, pl.ds(6, 1), :] = walls[0, plane, edge, :]
+        corners_out[diagonal, pl.ds(7, 1), :] = walls[0, plane, beside, :]
         corners.append(
             send(corners_out.at[diagonal], corners_in.at[diagonal],
                  halo_send.at[0, 4 + diagonal], halo_recv.at[0, 4 + diagonal], dx, dz)
@@ -276,34 +296,38 @@
 
     def wall_from(number, x):
         cx, cy, cz = VELOCITIES[number]
-        return walls[(0, 1, 2)[cy], 1 + x - cx, pl.ds(TOP - cz, extent_z), :] > 0
+        return walls[(0, 1, 2)[cy], 1 + x - cx, pl.ds(TOP - 1 - cz, wide), :] > 0
 
     def second_collision(k, carry):
         x = lax.rem(k + 1, extent_x)
 
         @pl.when(k == extent_x - 2)
         def _():
-            for copy in x_sides + corners:
+            for copy in x_masks + x_sides + corners:
                 copy.wait_recv()
             for diagonal, (cx, cz) in enumerate(DIAGONALS):
+                beside, further = halo_rows(cz)
                 plane = 0 if cx > 0 else extent_x + 1
-                row = pl.ds(TOP - 1 if cz > 0 else TOP + extent_z, 1)
-                rolled[DIAGONAL_SLOT[diagonal], plane, row, :] = corners_in[diagonal, pl.ds(0, 1), :]
-                walls[0, plane, row, :] = corners_in[diagonal, pl.ds(1, 1), :]
+                for order in range(5):
+                    rolled[X_FIRST[cx] + order, plane, beside, :] = corners_in[diagonal, pl.ds(order, 1), :]
+                rolled[DIAGONAL_SLOT[diagonal], plane, further, :] = corners_in[diagonal, pl.ds(5, 1), :]
+                walls[0, plane, beside, :] = corners_in[diagonal, pl.ds(6, 1), :]
+                walls[0, plane, further, :] = corners_in[diagonal, pl.ds(7, 1), :]
             for plane in (0, extent_x + 1):
                 shift_walls(plane)
 
-        fluid = walls[0, 1 + x, inner, :] > 0
+        region = pl.ds(TOP - 1, wide)
+        fluid = walls[0, 1 + x, region, :] > 0
         owned = []
         for number in range(19):
             if VELOCITIES[number][1]:
-                owned.append(plain[number, x])
+                owned.append(plain[number, x, region, :])
             else:
-                owned.append(rolled[SLOT[number], 1 + x, inner, :])
+                owned.append(rolled[SLOT[number], 1 + x, region, :])
         f = [owned[0]]
         for number in range(1, 19):
             cx, cy, cz = VELOCITIES[number]
-            value = rolled[SLOT[number], 1 + x - cx, pl.ds(TOP - cz, extent_z), :]
+            value = rolled[SLOT[number], 1 + x - cx, pl.ds(TOP - 1 - cz, wide), :]
             arrived = jnp.where(wall_from(number, x), value, owned[OPPOSITES[number]])
             f.append(jnp.where(fluid, arrived, owned[number]))
         g = collide(f, fluid)
@@ -318,30 +342,34 @@
             leaving[cx, cz] = leaving[cx, cz] + value if (cx, cz) in leaving else value
             value = jnp.where(wall_from(number, x), 0.0, g[OPPOSITES[number]])
             turned_back[cx] = turned_back[cx] + value if cx in turned_back else value
-        for cx, keep in ((1, ahead), (-1, behind), (0, None)):
-            total = leaving[cx, 0]
-            for cz in (1, -1):
-                value = leaving[cx, cz]
-                rims[RIM[cx, cz], x] = edge_of(value, cz)
-                moved = pltpu.roll(value, cz % extent_z, 0)
-                total = total + jnp.where(rows == (0 if cz > 0 else extent_z - 1), 0.0, moved)
-            if keep is None:
-                density[x] = (g[0] + total) + (turned_back[0] + turned_back[1] + turned_back[-1])
-            else:
-                keep[x] = total
-        forward[x] = turned_back[1] - turned_back[-1]
+        stay = slice(1, 1 + extent_z)
+        leaving[0, 0] = leaving[0, 0] + g[0] + (turned_back[0] + turned_back[1] + turned_back[-1])
+        for cx, keep in ((1, ahead), (-1, behind), (0, density)):
+            keep[x] = leaving[cx, 0][stay] + leaving[cx, 1][:extent_z] + leaving[cx, -1][2:]
+        forward[x] = (turned_back[1] - turned_back[-1])[stay]
         return carry
 
     for copy in z_sides:
         copy.wait_recv()
-    for side, cz in enumerate((1, -1)):
-        row = pl.ds(TOP - 1 if cz > 0 else TOP + extent_z, 1)
-        for x in range(extent_x):
+    def unpack(x, carry):
+        for side, cz in enumerate((1, -1)):
+            beside, further = halo_rows(cz)
+            for number in range(19):
+                value = edges_in[side, x, pl.ds(number, 1), :]
+                cy = VELOCITIES[number][1]
+                if cy:
+                    plain[number, x, beside, :] = value
+                    value = pltpu.roll(value, cy % height, 1)
+                rolled[SLOT[number], 1 + x, beside, :] = value
             for order in range(5):
-                rolled[(Z_FIRST[cz] + order) % 16, 1 + x, row, :] = edges_in[
-                    side, pl.ds(order * extent_x + x, 1), :
+                rolled[(Z_FIRST[cz] + order) % 16, 1 + x, further, :] = edges_in[
+                    side, x, pl.ds(19 + order, 1), :
                 ]
-            walls[0, 1 + x, row, :] = edges_in[side, pl.ds(5 * extent_x + x, 1), :]
+            walls[0, 1 + x, beside, :] = edges_in[side, x, pl.ds(24, 1), :]
+            walls[0, 1 + x, further, :] = edges_in[side, x, pl.ds(25, 1), :]
+        return carry
+
+    lax.fori_loop(0, extent_x, unpack, 0)
 
     def shift_inner(plane, carry):
         shift_walls(plane)
@@ -350,24 +378,6 @@
     lax.fori_loop(1, 1 + extent_x, shift_inner, 0)
     lax.fori_loop(0, extent_x, second_collision, 0)
 
-    rim_copies = []
-    for side, dz in enumerate((1, -1)):
-        for x in range(extent_x):
-            total, along = rims[RIM[0, dz], x], None
-            if x > 0:
-                forth = rims[RIM[1, dz], x - 1]
-                total, along = total + forth, forth
-            if x < last:
-                back = rims[RIM[-1, dz], x + 1]
-                total, along = total + back, -back if along is None else along - back
-            rims_out[side, pl.ds(x, 1), :] = total
-            rims_out[side, pl.ds(extent_x + x, 1), :] = along
-        rims_out[side, pl.ds(2 * extent_x, 1), :] = rims[RIM[1, dz], last]
-        rims_out[side, pl.ds(2 * extent_x + 1, 1), :] = rims[RIM[-1, dz], 0]
-        rim_copies.append(
-            send(rims_out.at[side], rims_in.at[side],
-                 halo_send.at[1, side], halo_recv.at[1, side], 0, dz)
-        )
     for x in range(extent_x):
         total, along = density[x], forward[x]
         if x > 0:
@@ -376,15 +386,8 @@
             total, along = total + behind[x + 1], along - behind[x + 1]
         density[x] = total
         forward[x] = along
-    for copy in rim_copies:
-        copy.wait_recv()
-    for side, dz in enumerate((1, -1)):
-        row = pl.ds(0 if dz > 0 else extent_z - 1, 1)
-        for x in range(extent_x):
-            density[x, row, :] = density[x, row, :] + rims_in[side, pl.ds(x, 1), :]
-            forward[x, row, :] = forward[x, row, :] + rims_in[side, pl.ds(extent_x + x, 1), :]
-        ahead[last, row, :] = ahead[last, row, :] + rims_in[side, pl.ds(2 * extent_x, 1), :]
-        behind[0, row, :] = behind[0, row, :] + rims_in[side, pl.ds(2 * extent_x + 1, 1), :]
+
+    halo_copies = x_sides + x_masks + z_sides + corners
 
     def is_fluid(plane):
         return walls[0, plane, inner, :] > 0
@@ -405,7 +408,7 @@
             if x == last:
                 total, along = total + sums_in[1], along - sums_in[1]
             out_ref[x] = jnp.where(is_fluid(1 + x), along / total, 0.0)
-        for copy in rim_copies + sums:
+        for copy in halo_copies + sums:
             copy.wait_send()
 
     if spectral:
@@ -436,6 +439,8 @@
         got_x[mx] = sent_x[mx]
         table_copy.wait()
         first = weights[pl.ds(16, 128), :].astype(jnp.bfloat16)
+        for copy in halo_copies:
+            copy.wait_send()
         for copy in x_copies:
             copy.wait_recv()
         lane = lax.broadcasted_iota(jnp.int32, (16, 128), 1)
@@ -485,6 +490,8 @@
         got_z[mz] = sent_z[mz]
         second_high, second_low = halves(weights[pl.ds(144, 128), :])
         second_twice = jnp.concatenate([second_high, second_high], axis=0)
+        for copy in x_copies:
+            copy.wait_send()
         for copy in z_copies:
             copy.wait_recv()
         lines = got_z[...].reshape(128, 128).T
@@ -494,10 +501,8 @@
         ) + jnp.dot(high, second_low, preferred_element_type=jnp.float32)
         out_ref[0] = result[:, :64].reshape(16, 8, 64)
         out_ref[1] = result[:, 64:].reshape(16, 8, 64)
-        for copy in rim_copies + x_copies + z_copies:
+        for copy in z_copies:
             copy.wait_send()
-    for copy in x_sides + z_sides + corners:
-        copy.wait_send()
 
 
 def shards(populations, fluid_mask):
@@ -512,26 +517,22 @@
         table = jnp.zeros((8, 128), jnp.float32)
     f32 = jnp.float32
     padded = (extent_x + 2, extent_z + 2 * TOP, height)
-    edge_rows = 6 * extent_x
     dma = pltpu.SemaphoreType.DMA
     scratch = [
         pltpu.VMEM((extent_x, 19, extent_z, height), f32),
         pltpu.VMEM((extent_x, extent_z, height), jnp.int32),
         pltpu.VMEM((19,) + padded, f32),
-        pltpu.VMEM((19, extent_x, extent_z, height), f32),
+        pltpu.VMEM((19, extent_x) + padded[1:], f32),
         pltpu.VMEM((3,) + padded, f32),
-        pltpu.VMEM((2, edge_rows, height), f32),
-        pltpu.VMEM((2, edge_rows, height), f32),
-        pltpu.VMEM((4, 2, height), f32),
-        pltpu.VMEM((4, 2, height), f32),
+        pltpu.VMEM((2, extent_x, 26, height), f32),
+        pltpu.VMEM((2, extent_x, 26, height), f32),
+        pltpu.VMEM((4, 8, height), f32),
+        pltpu.VMEM((4, 8, height), f32),
         pltpu.VMEM((2, extent_z, height), f32),
-        pltpu.VMEM((2, 2 * extent_x + 2, height), f32),
-        pltpu.VMEM((2, 2 * extent_x + 2, height), f32),
         pltpu.VMEM((extent_x, extent_z, height), f32),
         pltpu.VMEM((extent_x, extent_z, height), f32),
         pltpu.VMEM((extent_x, extent_z, height), f32),
         pltpu.VMEM((extent_x, extent_z, height), f32),
-        pltpu.VMEM((6, extent_x, 1, height), f32),
         dma((extent_x + 1,)),
         dma((2, 8)),
         dma((2, 8)),

time: 22.8 us -> 21.3 us (0.934)
  Pallas kernels: 22 us -> 20.5 us
    pallas_call x1, Pallas kernels: 22 us -> 20.5 us  [shards(): pl.pallas_call(functools.partial(kernel, spectral), out_shape=out_shape,...]
where the time goes in v7:
time: 21.3 us; the launch traced here: 21.1 us
  Pallas kernels  20.5 us (96%)
  local copies, waits for them, and re-layouts  0.66 us (3%)
    pallas_call x1, Pallas kernels, shards(): pl.pallas_call(functools.partial(kernel, spectral), out_shape=out_shape,...  20.5 us
    unnamed x1, local copies, waits for them, and re-layouts  0.66 us

profile of v7, /device:TPU:0, one launch (start us, length us, event | category | flops | bytes accessed | tf_op | source)
XLA Modules:
  0.0 21.1 jit_solution(13710786716010552544)
XLA Ops:
  0.0 20.5 %shard_map.37 = f32[2,16,8,64]{3,2,1,0:T(8,128)S(1)} custom-call(f32[19,4,16,128]{3,2,1,0:T(8,128)} %populations.1, s32[4,16,128]{2,1,0:T(8,128)} %fluid_mask.1, f32[272,128]{1,0:T(8,128)} %constant.2.clone.table), custom_call_target="tpu_custom_call" | custom-call | tf_op jit(solution)/shard_map/pallas_call | solution.py:560
  20.5 0.7 %copy.5 = f32[2,16,8,64]{3,2,1,0:T(8,128)} copy(f32[2,16,8,64]{3,2,1,0:T(8,128)S(1)} %shard_map.37) | data formatting | bytes 131072

commit v8 on v7

--- a/solution.py
+++ b/solution.py
@@ -167,11 +167,6 @@
     def fetch(x):
         return pltpu.make_async_copy(populations.at[:, x], held.at[x], in_sem.at[x])
 
-    mask_copy = pltpu.make_async_copy(fluid_mask, mask_i, in_sem.at[extent_x])
-    mask_copy.start()
-    for k in range(extent_x):
-        fetch((extent_x - k) % extent_x).start()
-
     barrier = pltpu.get_barrier_semaphore()
     partners = [(shifted_x(dx), shifted_z(dz)) for dx, dz in SIDES + DIAGONALS]
     if spectral:
@@ -179,6 +174,10 @@
         partners += [(mx, shifted_z(p)) for p in range(2, count_z - 1)]
     for partner in partners:
         pl.semaphore_signal(barrier, inc=1, device_id=partner, device_id_type=MESH)
+    mask_copy = pltpu.make_async_copy(fluid_mask, mask_i, in_sem.at[extent_x])
+    mask_copy.start()
+    for k in range(extent_x):
+        fetch((extent_x - k) % extent_x).start()
     if spectral:
         table_copy = pltpu.make_async_copy(table, weights, table_sem.at[0])
         table_copy.start()
@@ -224,6 +223,29 @@
                    mask_send.at[side], mask_recv.at[side], dx, 0)
         )
 
+    def send_along_x():
+        odd = lax.rem(mx, 2)
+        for up in (odd, 1 - odd):
+            here, there = 1 + up * last, (1 - up) * (extent_x + 1)
+            side, start = 1 - up, X_FIRST[-1] * (1 - up)
+            target = (shifted_x(2 * up - 1), mz)
+            pltpu.make_async_remote_copy(
+                src_ref=rolled.at[pl.ds(start, 5), here, inner],
+                dst_ref=rolled.at[pl.ds(start, 5), there, inner],
+                send_sem=halo_send.at[0, side],
+                recv_sem=halo_recv.at[0, side],
+                device_id=target,
+                device_id_type=MESH,
+            ).start()
+            pltpu.make_async_remote_copy(
+                src_ref=walls.at[0, here, inner],
+                dst_ref=walls.at[0, there, inner],
+                send_sem=mask_send.at[side],
+                recv_sem=mask_recv.at[side],
+                device_id=target,
+                device_id_type=MESH,
+            ).start()
+
     mask_copy.wait()
     for x in range(extent_x):
         walls[0, 1 + x, inner, :] = mask_i[x].astype(jnp.float32)
@@ -243,8 +265,7 @@
         @pl.when(k == 1)
         def _():
             pl.semaphore_wait(barrier, len(partners))
-            for copy in x_sides + x_masks:
-                copy.start()
+            send_along_x()
 
         return carry
 
@@ -424,13 +445,17 @@
         parts.append(jnp.where(is_fluid(extent_x), forward[last], 0.0))
         sent_x[...] = jnp.concatenate(parts, axis=0).T.reshape(8, 16, 128)
         x_copies = []
-        for p in range(1, count_x):
-            there = shifted_x(p)
+        lower = jnp.where(mx < count_x // 2, 1, 0)
+        for order in range(count_x - 1):
+            down = count_x - 1 - order
+            down = down - jnp.where(down <= mx, 1, 0)
+            up = order + jnp.where(order >= mx, 1, 0)
+            there = lower * down + (1 - lower) * up
             copy = pltpu.make_async_remote_copy(
                 src_ref=sent_x.at[there],
                 dst_ref=got_x.at[mx],
-                send_sem=x_send.at[p],
-                recv_sem=x_recv.at[p],
+                send_sem=x_send.at[order],
+                recv_sem=x_recv.at[mx],
                 device_id=(there, mz),
                 device_id_type=MESH,
             )
@@ -441,8 +466,16 @@
         first = weights[pl.ds(16, 128), :].astype(jnp.bfloat16)
         for copy in halo_copies:
             copy.wait_send()
-        for copy in x_copies:
-            copy.wait_recv()
+        for p in range(1, count_x):
+            source = shifted_x(p)
+            pltpu.make_async_remote_copy(
+                src_ref=sent_x.at[source],
+                dst_ref=got_x.at[source],
+                send_sem=x_send.at[0],
+                recv_sem=x_recv.at[source],
+                device_id=(source, mz),
+                device_id_type=MESH,
+            ).wait_recv()
         lane = lax.broadcasted_iota(jnp.int32, (16, 128), 1)
         head, tail = lane < 16, lane >= 48
         got = [got_x[s] for s in range(8)]

time: 21.3 us -> 21.2 us (level)
  no operation moved by 1% of the time
where the time goes in v8:
time: 21.2 us; the launch traced here: 21.1 us
  Pallas kernels  20.4 us (96%)
  local copies, waits for them, and re-layouts  0.66 us (3%)
    pallas_call x1, Pallas kernels, shards(): pl.pallas_call(functools.partial(kernel, spectral), out_shape=out_shape,...  20.4 us
    unnamed x1, local copies, waits for them, and re-layouts  0.66 us

profile of v8, /device:TPU:0, one launch (start us, length us, event | category | flops | bytes accessed | tf_op | source)
XLA Modules:
  0.0 21.1 jit_solution(817931831684690010)
XLA Ops:
  0.0 20.4 %shard_map.37 = f32[2,16,8,64]{3,2,1,0:T(8,128)S(1)} custom-call(f32[19,4,16,128]{3,2,1,0:T(8,128)} %populations.1, s32[4,16,128]{2,1,0:T(8,128)} %fluid_mask.1, f32[272,128]{1,0:T(8,128)} %constant.2.clone.table), custom_call_target="tpu_custom_call" | custom-call | tf_op jit(solution)/shard_map/pallas_call | solution.py:593
  20.4 0.7 %copy.5 = f32[2,16,8,64]{3,2,1,0:T(8,128)} copy(f32[2,16,8,64]{3,2,1,0:T(8,128)S(1)} %shard_map.37) | data formatting | bytes 131072

commit v9 on v7

--- a/solution.py
+++ b/solution.py
@@ -36,13 +36,15 @@
 BODY_FORCE = 0.0001
 SPEED_UNIT = 0.05
 
-CHAIN = (13, 1, 7, 9, 11, 5, 15, 18, 14, 2, 8, 10, 12, 6, 16, 17, 0, 3, 4)
-SLOT = {number: CHAIN.index(number) for number in CHAIN}
-X_FIRST = {1: 0, -1: 8}
-Z_FIRST = {1: 4, -1: 12}
+X_GROUP = {1: (13, 1, 7, 9, 11), -1: (14, 2, 8, 10, 12)}
+Z_GROUP = {1: (11, 5, 15, 18, 14), -1: (12, 6, 16, 17, 13)}
+CHAIN = (-1,) + X_GROUP[1] + (5, 15, 18, 6, 16, 17, 0, 3, 4) + X_GROUP[-1] + (-1,)
+SLOT = {number: CHAIN.index(number) for number in range(19)}
+X_FIRST = {1: 0, -1: len(CHAIN) - 6}
+SOLIDITY = {1: 0, -1: len(CHAIN) - 1}
 SIDES = ((1, 0), (-1, 0), (0, 1), (0, -1))
 DIAGONALS = ((1, 1), (1, -1), (-1, 1), (-1, -1))
-DIAGONAL_SLOT = (4, 0, 8, 12)
+DIAGONAL_MOVER = (11, 13, 14, 12)
 TOP = 8
 MESH = pl.DeviceIdType.MESH
 
@@ -147,10 +149,10 @@
 def kernel(spectral, populations, fluid_mask, table, *rest):
     (out_ref, held, mask_i, rolled, plain, walls, edges_out, edges_in, corners_out, corners_in,
      sums_in, density, forward, ahead, behind,
-     in_sem, halo_send, halo_recv, mask_send, mask_recv) = rest[:20]
+     in_sem, halo_send, halo_recv) = rest[:18]
     if spectral:
         (sent_x, got_x, left, sent_z, got_z, weights,
-         table_sem, x_send, x_recv, z_send, z_recv) = rest[20:]
+         table_sem, x_send, x_recv, z_send, z_recv) = rest[18:]
     extent_x, extent_z, height = fluid_mask.shape
     last = extent_x - 1
     count_x, count_z = lax.axis_size("gx"), lax.axis_size("gz")
@@ -211,22 +213,36 @@
         copy.start()
         return copy
 
-    x_sides, x_masks = [], []
+    x_sides = []
     for side, dx in enumerate((1, -1)):
         here, there = (extent_x, 0) if dx > 0 else (1, extent_x + 1)
-        group = pl.ds(X_FIRST[dx], 5)
+        group = pl.ds(X_FIRST[dx], 6)
         x_sides.append(
             remote(rolled.at[group, here, inner], rolled.at[group, there, inner],
                    halo_send.at[0, side], halo_recv.at[0, side], dx, 0)
         )
-        x_masks.append(
-            remote(walls.at[0, here, inner], walls.at[0, there, inner],
-                   mask_send.at[side], mask_recv.at[side], dx, 0)
-        )
+
+    def send_along_x():
+        odd = lax.rem(mx, 2)
+        for up in (odd, 1 - odd):
+            group = pl.ds(X_FIRST[-1] * (1 - up), 6)
+            pltpu.make_async_remote_copy(
+                src_ref=rolled.at[group, 1 + up * last, inner],
+                dst_ref=rolled.at[group, (1 - up) * (extent_x + 1), inner],
+                send_sem=halo_send.at[0, 1 - up],
+                recv_sem=halo_recv.at[0, 1 - up],
+                device_id=(shifted_x(2 * up - 1), mz),
+                device_id_type=MESH,
+            ).start()
 
     mask_copy.wait()
     for x in range(extent_x):
-        walls[0, 1 + x, inner, :] = mask_i[x].astype(jnp.float32)
+        solid = mask_i[x].astype(jnp.float32)
+        walls[0, 1 + x, inner, :] = solid
+        if x == last:
+            rolled[SOLIDITY[1], 1 + x, inner, :] = solid
+        if x == 0:
+            rolled[SOLIDITY[-1], 1 + x, inner, :] = solid
 
     def first_collision(k, carry):
         x = lax.rem(extent_x - k, extent_x)
@@ -243,8 +259,7 @@
         @pl.when(k == 1)
         def _():
             pl.semaphore_wait(barrier, len(partners))
-            for copy in x_sides + x_masks:
-                copy.start()
+            send_along_x()
 
         return carry
 
@@ -262,7 +277,7 @@
                 edges_out[side, x, pl.ds(number, 1), :] = value
             for order in range(5):
                 edges_out[side, x, pl.ds(19 + order, 1), :] = rolled[
-                    (Z_FIRST[cz] + order) % 16, 1 + x, beside, :
+                    SLOT[Z_GROUP[cz][order]], 1 + x, beside, :
                 ]
             edges_out[side, x, pl.ds(24, 1), :] = walls[0, 1 + x, edge, :]
             edges_out[side, x, pl.ds(25, 1), :] = walls[0, 1 + x, beside, :]
@@ -278,8 +293,8 @@
         edge, beside = edge_rows(dz)
         plane = extent_x if dx > 0 else 1
         for order in range(5):
-            corners_out[diagonal, pl.ds(order, 1), :] = rolled[X_FIRST[dx] + order, plane, edge, :]
-        corners_out[diagonal, pl.ds(5, 1), :] = rolled[DIAGONAL_SLOT[diagonal], plane, beside, :]
+            corners_out[diagonal, pl.ds(order, 1), :] = rolled[SLOT[X_GROUP[dx][order]], plane, edge, :]
+        corners_out[diagonal, pl.ds(5, 1), :] = rolled[SLOT[DIAGONAL_MOVER[diagonal]], plane, beside, :]
         corners_out[diagonal, pl.ds(6, 1), :] = walls[0, plane, edge, :]
         corners_out[diagonal, pl.ds(7, 1), :] = walls[0, plane, beside, :]
         corners.append(
@@ -303,14 +318,16 @@
 
         @pl.when(k == extent_x - 2)
         def _():
-            for copy in x_masks + x_sides + corners:
+            for copy in x_sides + corners:
                 copy.wait_recv()
+            for cx, plane in ((1, 0), (-1, extent_x + 1)):
+                walls[0, plane, inner, :] = rolled[SOLIDITY[cx], plane, inner, :]
             for diagonal, (cx, cz) in enumerate(DIAGONALS):
                 beside, further = halo_rows(cz)
                 plane = 0 if cx > 0 else extent_x + 1
                 for order in range(5):
-                    rolled[X_FIRST[cx] + order, plane, beside, :] = corners_in[diagonal, pl.ds(order, 1), :]
-                rolled[DIAGONAL_SLOT[diagonal], plane, further, :] = corners_in[diagonal, pl.ds(5, 1), :]
+                    rolled[SLOT[X_GROUP[cx][order]], plane, beside, :] = corners_in[diagonal, pl.ds(order, 1), :]
+                rolled[SLOT[DIAGONAL_MOVER[diagonal]], plane, further, :] = corners_in[diagonal, pl.ds(5, 1), :]
                 walls[0, plane, beside, :] = corners_in[diagonal, pl.ds(6, 1), :]
                 walls[0, plane, further, :] = corners_in[diagonal, pl.ds(7, 1), :]
             for plane in (0, extent_x + 1):
@@ -362,7 +379,7 @@
                     value = pltpu.roll(value, cy % height, 1)
                 rolled[SLOT[number], 1 + x, beside, :] = value
             for order in range(5):
-                rolled[(Z_FIRST[cz] + order) % 16, 1 + x, further, :] = edges_in[
+                rolled[SLOT[Z_GROUP[cz][order]], 1 + x, further, :] = edges_in[
                     side, x, pl.ds(19 + order, 1), :
                 ]
             walls[0, 1 + x, beside, :] = edges_in[side, x, pl.ds(24, 1), :]
@@ -387,7 +404,7 @@
         density[x] = total
         forward[x] = along
 
-    halo_copies = x_sides + x_masks + z_sides + corners
+    halo_copies = x_sides + z_sides + corners
 
     def is_fluid(plane):
         return walls[0, plane, inner, :] > 0
@@ -521,7 +538,7 @@
     scratch = [
         pltpu.VMEM((extent_x, 19, extent_z, height), f32),
         pltpu.VMEM((extent_x, extent_z, height), jnp.int32),
-        pltpu.VMEM((19,) + padded, f32),
+        pltpu.VMEM((len(CHAIN),) + padded, f32),
         pltpu.VMEM((19, extent_x) + padded[1:], f32),
         pltpu.VMEM((3,) + padded, f32),
         pltpu.VMEM((2, extent_x, 26, height), f32),
@@ -536,8 +553,6 @@
         dma((extent_x + 1,)),
         dma((2, 8)),
         dma((2, 8)),
-        dma((2,)),
-        dma((2,)),
     ]
     if spectral:
         scratch += [

time: 21.3 us -> 21.2 us (level)
  no operation moved by 1% of the time
where the time goes in v9:
time: 21.2 us; the launch traced here: 21.1 us
  Pallas kernels  20.4 us (96%)
  local copies, waits for them, and re-layouts  0.66 us (3%)
    pallas_call x1, Pallas kernels, shards(): pl.pallas_call(functools.partial(kernel, spectral), out_shape=out_shape,...  20.4 us
    unnamed x1, local copies, waits for them, and re-layouts  0.66 us

profile of v9, /device:TPU:0, one launch (start us, length us, event | category | flops | bytes accessed | tf_op | source)
XLA Modules:
  0.0 21.1 jit_solution(1136101042896991175)
XLA Ops:
  0.0 20.4 %shard_map.37 = f32[2,16,8,64]{3,2,1,0:T(8,128)S(1)} custom-call(f32[19,4,16,128]{3,2,1,0:T(8,128)} %populations.1, s32[4,16,128]{2,1,0:T(8,128)} %fluid_mask.1, f32[272,128]{1,0:T(8,128)} %constant.2.clone.table), custom_call_target="tpu_custom_call" | custom-call | tf_op jit(solution)/shard_map/pallas_call | solution.py:575
  20.4 0.7 %copy.5 = f32[2,16,8,64]{3,2,1,0:T(8,128)} copy(f32[2,16,8,64]{3,2,1,0:T(8,128)S(1)} %shard_map.37) | data formatting | bytes 131072

commit v10 on v9

--- a/solution.py
+++ b/solution.py
@@ -255,12 +255,6 @@
                 plain[number, x, inner, :] = value
                 value = pltpu.roll(value, cy % height, 1)
             rolled[SLOT[number], 1 + x, inner, :] = value
-
-        @pl.when(k == 1)
-        def _():
-            pl.semaphore_wait(barrier, len(partners))
-            send_along_x()
-
         return carry
 
     lax.fori_loop(0, extent_x, first_collision, 0)
@@ -283,12 +277,6 @@
             edges_out[side, x, pl.ds(25, 1), :] = walls[0, 1 + x, beside, :]
         return carry
 
-    lax.fori_loop(0, extent_x, pack, 0)
-    for side, cz in enumerate((1, -1)):
-        z_sides.append(
-            send(edges_out.at[side], edges_in.at[side],
-                 halo_send.at[0, 2 + side], halo_recv.at[0, 2 + side], 0, cz)
-        )
     for diagonal, (dx, dz) in enumerate(DIAGONALS):
         edge, beside = edge_rows(dz)
         plane = extent_x if dx > 0 else 1
@@ -297,9 +285,18 @@
         corners_out[diagonal, pl.ds(5, 1), :] = rolled[SLOT[DIAGONAL_MOVER[diagonal]], plane, beside, :]
         corners_out[diagonal, pl.ds(6, 1), :] = walls[0, plane, edge, :]
         corners_out[diagonal, pl.ds(7, 1), :] = walls[0, plane, beside, :]
+    lax.fori_loop(0, extent_x, pack, 0)
+    pl.semaphore_wait(barrier, len(partners))
+    send_along_x()
+    for diagonal, (dx, dz) in enumerate(DIAGONALS):
         corners.append(
             send(corners_out.at[diagonal], corners_in.at[diagonal],
                  halo_send.at[0, 4 + diagonal], halo_recv.at[0, 4 + diagonal], dx, dz)
+        )
+    for side, cz in enumerate((1, -1)):
+        z_sides.append(
+            send(edges_out.at[side], edges_in.at[side],
+                 halo_send.at[0, 2 + side], halo_recv.at[0, 2 + side], 0, cz)
         )
 
     around = lax.broadcasted_iota(jnp.int32, (extent_z + 2 * TOP, height), 1)

time: 21.2 us -> 21.2 us (level)
  no operation moved by 1% of the time
where the time goes in v10:
time: 21.2 us; the launch traced here: 21.1 us
  Pallas kernels  20.4 us (96%)
  local copies, waits for them, and re-layouts  0.66 us (3%)
    pallas_call x1, Pallas kernels, shards(): pl.pallas_call(functools.partial(kernel, spectral), out_shape=out_shape,...  20.4 us
    unnamed x1, local copies, waits for them, and re-layouts  0.66 us

profile of v10, /device:TPU:0, one launch (start us, length us, event | category | flops | bytes accessed | tf_op | source)
XLA Modules:
  0.0 21.1 jit_solution(3229964061069610194)
XLA Ops:
  0.0 20.4 %shard_map.37 = f32[2,16,8,64]{3,2,1,0:T(8,128)S(1)} custom-call(f32[19,4,16,128]{3,2,1,0:T(8,128)} %populations.1, s32[4,16,128]{2,1,0:T(8,128)} %fluid_mask.1, f32[272,128]{1,0:T(8,128)} %constant.2.clone.table), custom_call_target="tpu_custom_call" | custom-call | tf_op jit(solution)/shard_map/pallas_call | solution.py:572
  20.4 0.7 %copy.5 = f32[2,16,8,64]{3,2,1,0:T(8,128)} copy(f32[2,16,8,64]{3,2,1,0:T(8,128)S(1)} %shard_map.37) | data formatting | bytes 131072
